TPU v7x, 32 devices: a whole 2x2x4 slice. The times are simulated.
32 devices in a mesh: ad: 8 (over z, x), bn: 4 (over y, core).
Axes of the slice: x: 2, y: 2, z: 4, core: 2. Of those that a mesh axis runs over, the one named last changes fastest.
Arguments:
- hidden_in: bfloat16 [8192, 768], P(('ad', 'bn')), may hold values from -6 to 6
- lengths: int32 [32], P(('ad', 'bn')), may hold values from 16 to 256, as said below
- cotangent: bfloat16 [8192, 768], P(('ad', 'bn')), may hold values from -6 to 6
- w_qkv: bfloat16 [768, 2304], replicated, may hold values from -0.21875 to 0.21875
- w_out: bfloat16 [768, 768], replicated, may hold values from -1.75 to 1.75
- gain_attn: float32 [768], replicated, may hold values from 0.1 to 1.9
- w_ff_in: bfloat16 [768, 3072], replicated, may hold values from -0.21875 to 0.21875
- w_ff_out: bfloat16 [3072, 768], replicated, may hold values from -0.109375 to 0.109375
- gain_ff: float32 [768], replicated, may hold values from 0.1 to 1.9
- join_query: bfloat16 [768, 768], replicated, may hold values from -0.21875 to 0.21875
- join_key: bfloat16 [768, 768], replicated, may hold values from -0.21875 to 0.21875
- join_value: bfloat16 [768, 768], replicated, may hold values from -0.21875 to 0.21875
- adapt_down: bfloat16 [48, 16, 768], P('bn'), may hold values from -0.21875 to 0.21875
- adapt_up: bfloat16 [48, 16, 768], P('bn'), may hold values from -1.75 to 1.75
- gain_out: float32 [768], replicated, may hold values from 0.1 to 1.9
Outputs:
- output: float32 [8192, 768], P(('ad', 'bn'))
- grad_in: float32 [8192, 768], P(('ad', 'bn'))
- grad_w_qkv: float32 [768, 2304], P('bn', 'ad')
- grad_w_out: float32 [768, 768], P('bn', 'ad')
- grad_gain_attn: float32 [768], P('ad')
- grad_w_ff_in: float32 [768, 3072], P('bn', 'ad')
- grad_w_ff_out: float32 [3072, 768], P('bn', 'ad')
- grad_gain_ff: float32 [768], P('ad')
- grad_join_query: float32 [768, 768], P('bn', 'ad')
- grad_join_key: float32 [768, 768], P('bn', 'ad')
- grad_join_value: float32 [768, 768], P('bn', 'ad')
- grad_adapt_down: float32 [48, 16, 768], P('bn', None, 'ad')
- grad_adapt_up: float32 [48, 16, 768], P('bn', None, 'ad')
- grad_gain_out: float32 [768], P('ad')
Inputs may be any that keep to these rules, and one draw needn't show every extreme that they name: Each sequence holds its real tokens in the first lengths slots of its 256; in every draw one sequence, chosen by the seed, fills all its slots.
All inputs are finite; a program needn't handle non-finite values.
Results may differ from a plain program's by a relative error of at most 0.04.
Values may be sent and summed in bfloat16 or wider, within the bound.
A program may use at most 192 MiB of HBM per device.

v0:
```python
import functools
import math

import jax
import jax.numpy as jnp
from jax import lax
from jax.experimental import pallas as pl
from jax.experimental.pallas import tpu as pltpu
from jax.sharding import PartitionSpec as P

H = 12


epsilon = 1e-06
masked_value = -1000000000.0
MESH = pl.DeviceIdType.MESH


def layer_norm(values, gain):
    center = values - jnp.mean(values, -1, keepdims=True)
    spread = jnp.mean(center * center, -1, keepdims=True)
    return center * lax.rsqrt(spread + epsilon) * gain


def gelu_exact(values):
    return jax.nn.gelu(values, approximate=False)


def matmul(left, right):
    return jnp.dot(left, right, preferred_element_type=jnp.float32)


def matmul_t(left, right):
    return lax.dot_general(
        left, right, (((1,), (1,)), ((), ())), preferred_element_type=jnp.float32
    )


def matmul_tn(left, right):
    return lax.dot_general(
        left, right, (((0,), (0,)), ((), ())), preferred_element_type=jnp.float32
    )


def adapter_forward(hidden, probe_rows, down_flat, up_flat, adapters):
    row_count, model_width = hidden.shape
    inner_pre = matmul_t(hidden, down_flat)
    active = gelu_exact(inner_pre)
    weigh_rows = matmul_t(probe_rows, up_flat)
    logits = jnp.sum((active * weigh_rows).reshape(row_count, -1, adapters), 1) / math.sqrt(
        model_width
    )
    shares = jax.nn.softmax(logits, -1)
    mixing = (
        (shares[:, None, :] * active.reshape(row_count, -1, adapters))
        .reshape(row_count, -1)
        .astype(jnp.bfloat16)
    )
    return (mixing, (inner_pre, active, weigh_rows, shares))


def adapter_backward(kept_state, up_flat, mix_grad, adapters):
    inner_pre, active, weigh_rows, shares = kept_state
    row_count, model_width = mix_grad.shape
    score_scale = 1.0 / math.sqrt(model_width)
    mix_in = matmul_t(mix_grad, up_flat).reshape(row_count, -1, adapters)
    active_three = active.reshape(row_count, -1, adapters)
    weigh_three = weigh_rows.reshape(row_count, -1, adapters)
    share_grad = jnp.sum(mix_in * active_three, 1)
    logit_grad = shares * (share_grad - jnp.sum(shares * share_grad, -1, keepdims=True))
    act_grad = mix_in * shares[:, None, :] + logit_grad[:, None, :] * score_scale * weigh_three
    weigh_grad = (
        (logit_grad[:, None, :] * score_scale * active_three)
        .reshape(row_count, -1)
        .astype(jnp.bfloat16)
    )
    unused, gelu_back = jax.vjp(gelu_exact, inner_pre)
    inner_grad = gelu_back(act_grad.reshape(row_count, -1))[0].astype(jnp.bfloat16)
    return (inner_grad, weigh_grad)


PIECE = 48
SLOTS = 5
LAG_TWO = 4
LAG_THREE = 6
LAG_FOUR = 8
UNITS = (
    ((0, 8),),
    ((1, 9), (2, 10)),
    ((3, 11),),
    ((4, 12),),
    ((5, 7),),
    ((6, 3),),
    ((6, 4),),
    ((6, 5),),
    ((6, 6),),
    ((8, 2),),
    ((9, 2),),
    ((10, 2),),
    ((11, 2),),
    ((7, 1),),
    ((12, 0),),
    ((13, 0),),
    ((14, 0),),
)


def flip(index, bit):
    return index + bit - 2 * bit * ((index // bit) % 2)


def normal_parts(values):
    cdf = 0.5 * (1.0 + lax.erf(values * (1.0 / math.sqrt(2.0))))
    density = jnp.exp(values * values * -0.5) * (1.0 / math.sqrt(2.0 * math.pi))
    return cdf, density


def layer_kernel(
    heads,
    adapters,
    hidden,
    lengths,
    cotangent,
    w_qkv,
    w_out,
    gain_attn,
    w_ff_in,
    w_ff_out,
    gain_ff,
    join_query,
    join_key,
    join_value,
    adapt_down,
    adapt_up,
    gain_out,
    output,
    grad_in,
    sums,
    gain_sums,
    rows,
    rows_ff,
    rows_qkv,
    rows_sib,
    cols,
    cols_sib,
    ring,
    banks,
    acc,
    acc_two,
    wide,
    acc_t,
    acc_t_two,
    active,
    bank_slope,
    second,
    norm_one,
    norm_two,
    slope,
    qkv_t,
    probs,
    low_tmp,
    low_tmp_two,
    stat,
    stat_one,
    stat_two,
    gain_col,
    part,
    recv_one,
    recv_two,
    recv_three,
    gain_sum,
    gain_from,
    ring_sem,
    local_sem,
    bank_send,
    bank_recv,
    row_send,
    row_recv,
    col_send,
    col_recv,
    one_send,
    one_recv,
    two_send,
    two_recv,
    three_send,
    three_recv,
    last_send,
    last_recv,
    gain_send,
    gain_recv,
):
    low = jnp.bfloat16
    tokens, width = hidden.shape
    half_width = width // 2
    blocks = rows.shape[1] * rows.shape[2] * rows.shape[3]
    ad = lax.axis_index("ad")
    bn = lax.axis_index("bn")
    x, z = ad % 2, ad // 2
    core, y = bn % 2, bn // 2
    sibling = (ad, flip(bn, 1))
    x_mate = (flip(ad, 1), bn)
    y_mate = (ad, flip(bn, 2))
    z_index = [flip(z, 1), flip(z, 2), flip(flip(z, 1), 2)]
    z_mates = [(zz * 2 + x, bn) for zz in z_index]
    other_core, other_x, other_y = 1 - core, 1 - x, 1 - y

    loads = [(w_qkv.at[:, pl.ds(k * width, width)]) for k in range(3)] + [w_out]
    for k in range(4):
        loads.append(w_ff_in.at[:, pl.ds(k * width, width)])
        loads.append(w_ff_out.at[pl.ds(k * width, width), :])
    loads += [join_query, join_key, join_value]
    for k in range(4):
        loads.append(w_ff_out.at[pl.ds(k * width, width), :])
        loads.append(w_ff_in.at[:, pl.ds(k * width, width)])
    loads += [w_out] + [w_qkv.at[:, pl.ds(k * width, width)] for k in range(3)]
    free_slots = list(range(SLOTS))
    in_flight = []
    next_load = [0]

    def fill():
        while free_slots and next_load[0] < len(loads):
            slot = free_slots.pop(0)
            copy = pltpu.make_async_copy(loads[next_load[0]], ring.at[slot], ring_sem.at[slot])
            copy.start()
            in_flight.append((slot, copy))
            next_load[0] += 1

    def take():
        slot, copy = in_flight.pop(0)
        copy.wait()
        return slot

    def release(slot):
        free_slots.append(slot)
        fill()

    fill()
    bank_own = []
    for i, bank in enumerate((adapt_down, adapt_up)):
        bank_own.append(pltpu.make_async_copy(bank, banks.at[i, bn], local_sem.at[i]))
        bank_own[i].start()

    barrier = pltpu.get_barrier_semaphore()
    for mate in [sibling, x_mate, y_mate] + z_mates:
        pl.semaphore_signal(barrier, inc=1, device_id=mate, device_id_type=MESH)
    pl.semaphore_wait(barrier, 6)

    started = []

    def send(source, target, send_sem, recv_sem, mate):
        copy = pltpu.make_async_remote_copy(
            src_ref=source,
            dst_ref=target,
            send_sem=send_sem,
            recv_sem=recv_sem,
            device_id=mate,
            device_id_type=MESH,
        )
        copy.start()
        started.append(copy)
        return copy

    bank_sib, bank_y, bank_far = [], [], []
    for i, bank in enumerate((adapt_down, adapt_up)):
        bank_y.append(
            send(bank, banks.at[i, bn], bank_send.at[i, 1], bank_recv.at[i, 1], y_mate)
        )
    for i, bank in enumerate((adapt_down, adapt_up)):
        bank_sib.append(
            send(bank, banks.at[i, bn], bank_send.at[i, 0], bank_recv.at[i, 0], sibling)
        )

    def row_views(index):
        if index < 8:
            return rows.at[index]
        if index < 12:
            return rows_ff.at[:, :, index - 8]
        return rows_qkv.at[:, :, index - 12]

    def row_half(index, side):
        if index < 8:
            piece = rows[index, :, side, core]
        elif index < 12:
            piece = rows_ff[:, side, index - 8, core]
        else:
            piece = rows_qkv[:, side, index - 12, core]
        return piece.reshape(4 * PIECE, tokens)

    def col_ref(index):
        return hidden if index == 0 else cols.at[index - 1]

    row_copies, col_copies = {}, {}
    arrived = set()

    def share_row(index):
        row_copies[index] = send(
            row_views(index).at[:, :, other_core],
            rows_sib.at[index],
            row_send.at[index],
            row_recv.at[index],
            sibling,
        )

    def share_col(index):
        col_copies[index] = send(
            col_ref(index),
            cols_sib.at[index],
            col_send.at[index],
            col_recv.at[index],
            sibling,
        )

    one, two, three, last = {}, {}, {}, {}
    units = len(UNITS)

    def half(unit, side):
        total = None
        for left, right in UNITS[unit]:
            if (0, left) not in arrived:
                row_copies[left].wait_recv()
                arrived.add((0, left))
            if (1, right) not in arrived:
                col_copies[right].wait_recv()
                arrived.add((1, right))
            term = matmul(row_half(left, side), col_ref(right)[...])
            term += matmul(
                rows_sib[left, :, side].reshape(4 * PIECE, tokens), cols_sib[right]
            )
            total = term if total is None else total + term
        total = total.astype(low).reshape(4, PIECE, width)
        part[unit, 0, side] = total[:, :, :half_width]
        part[unit, 1, side] = total[:, :, half_width:]

    def stage_one(unit):
        if unit % 2 == 0:
            half(unit, other_x)
            one[unit] = send(
                part.at[unit, :, other_x],
                recv_one.at[unit],
                one_send.at[unit],
                one_recv.at[unit],
                x_mate,
            )
            half(unit, x)
        else:
            half(unit, 0)
            half(unit, 1)
            one[unit] = send(
                part.at[unit, other_y],
                recv_one.at[unit],
                one_send.at[unit],
                one_recv.at[unit],
                y_mate,
            )

    def add_low(left, right):
        return (left.astype(jnp.float32) + right.astype(jnp.float32)).astype(low)

    def stage_two(unit):
        one[unit].wait_recv()
        if unit % 2 == 0:
            part[unit, other_y, x] = add_low(part[unit, other_y, x], recv_one[unit, other_y])
            two[unit] = send(
                part.at[unit, other_y, x],
                recv_two.at[unit],
                two_send.at[unit],
                two_recv.at[unit],
                y_mate,
            )
            part[unit, y, x] = add_low(part[unit, y, x], recv_one[unit, y])
        else:
            part[unit, y, other_x] = add_low(part[unit, y, other_x], recv_one[unit, other_x])
            two[unit] = send(
                part.at[unit, y, other_x],
                recv_two.at[unit],
                two_send.at[unit],
                two_recv.at[unit],
                x_mate,
            )
            part[unit, y, x] = add_low(part[unit, y, x], recv_one[unit, x])

    def stage_three(unit):
        two[unit].wait_recv()
        part[unit, y, x] = add_low(part[unit, y, x], recv_two[unit])
        three[unit] = [
            send(
                part.at[unit, y, x, z_index[k]],
                recv_three.at[unit, k],
                three_send.at[unit, k],
                three_recv.at[unit, k],
                z_mates[k],
            )
            for k in range(3)
        ]

    def stage_four(unit):
        total = part[unit, y, x, z].astype(jnp.float32)
        for k in range(3):
            three[unit][k].wait_recv()
            total += recv_three[unit, k].astype(jnp.float32)
        sums[unit, core] = total.astype(low)
        last[unit] = send(
            sums.at[unit, core],
            sums.at[unit, core],
            last_send.at[unit],
            last_recv.at[unit],
            sibling,
        )

    def reduce_step(step):
        if step < units:
            stage_one(step)
        if 0 <= step - LAG_TWO < units:
            stage_two(step - LAG_TWO)
        if 0 <= step - LAG_THREE < units:
            stage_three(step - LAG_THREE)
        if 0 <= step - LAG_FOUR < units:
            stage_four(step - LAG_FOUR)

    step_rows = 32
    row_steps = tokens // step_rows

    def over_rows(body, init=0):
        def step(i, carry):
            return body(pl.ds(pl.multiple_of(i * step_rows, step_rows), step_rows), i, carry)

        return lax.fori_loop(0, row_steps, step, init)

    def over_pieces(body, init=0):
        return lax.fori_loop(0, blocks, body, init)

    def spot(p):
        return p // 4, (p // 2) % 2, p % 2

    def put_t(index, value):
        rows[index] = value.reshape(4, 2, 2, PIECE, tokens)

    def get_t(index):
        return rows[index].reshape(width, tokens)

    def fold(value):
        return value.reshape(PIECE // 8, 8, tokens).sum(0)

    share_col(0)
    length = lengths[0]
    for k in range(3):
        slot = take()
        value = matmul(hidden[...], ring[slot])
        release(slot)
        if k == 0:
            value = value * 0.125
        qkv_t[pl.ds(k * width, width), :] = value.astype(low).T
    size = width // heads

    def head_rows(k, head):
        return pl.ds(pl.multiple_of(k * width + head * size, size), size)

    valid_keys = lax.broadcasted_iota(jnp.int32, (tokens, tokens), 0) < length

    def head_forward(head, carry):
        scores = matmul_tn(qkv_t[head_rows(1, head), :], qkv_t[head_rows(0, head), :])
        scores = jnp.where(valid_keys, scores, masked_value)
        scores = jnp.exp(scores - jnp.max(scores, 0, keepdims=True))
        share = (scores * (1.0 / jnp.sum(scores, 0, keepdims=True))).astype(low)
        probs[head] = share
        context = matmul(qkv_t[head_rows(2, head), :], share)
        low_tmp_two[pl.ds(pl.multiple_of(head * size, size), size), :] = context.astype(low)
        return carry

    lax.fori_loop(0, heads, head_forward, 0)
    cols[0] = low_tmp_two[...].T
    share_col(1)
    slot = take()
    acc[...] = matmul(cols[0], ring[slot])
    release(slot)

    def norm_rows(total):
        center = total - jnp.mean(total, -1, keepdims=True)
        rstd = lax.rsqrt(jnp.mean(center * center, -1, keepdims=True) + epsilon)
        return center * rstd, rstd

    def norm_first(r, i, carry):
        normed, rstd = norm_rows(hidden[r, :].astype(jnp.float32) + acc[r, :])
        stat[r, :] = jnp.broadcast_to(rstd, (step_rows, 128))
        low_tmp[r, :] = normed.astype(low)
        one_rows = normed * gain_attn[...]
        wide[r, :] = one_rows
        cols[1, r, :] = one_rows.astype(low)
        return carry

    over_rows(norm_first)
    share_col(2)
    norm_one[...] = low_tmp[...].T.reshape(blocks, PIECE, tokens)
    stat_one[...] = stat[...].T[:8]

    for k in range(4):
        slot = take()
        acc[...] = matmul(cols[1], ring[slot])
        release(slot)
        unit_base = 2 + (k % 2) * 2
        lanes = pl.ds((k // 2) * half_width, half_width)

        def gelu_rows(r, i, carry):
            before = acc[r, :]
            cdf, density = normal_parts(before)
            act = (before * cdf).astype(low)
            low_tmp[r, :] = act
            cols[unit_base, r, lanes] = act[:, :half_width]
            cols[unit_base + 1, r, lanes] = act[:, half_width:]
            cols[9, r, :] = (cdf + before * density).astype(low)
            return carry

        over_rows(gelu_rows)
        slope[pl.ds(k * blocks, blocks)] = cols[9].T.reshape(blocks, PIECE, tokens)
        slot = take()
        value = matmul(low_tmp[...], ring[slot])
        release(slot)
        acc_two[...] = value if k == 0 else acc_two[...] + value
        if k == 1:
            for i in range(2):
                bank_y[i].wait_recv()
                far = flip(bn, 2)
                bank_far.append(
                    send(
                        banks.at[i, far],
                        banks.at[i, far],
                        bank_send.at[i, 2],
                        bank_recv.at[i, 2],
                        sibling,
                    )
                )
    for index in range(3, 7):
        share_col(index)

    def norm_second(r, i, carry):
        normed, rstd = norm_rows(wide[r, :] + acc_two[r, :])
        stat[r, :] = jnp.broadcast_to(rstd, (step_rows, 128))
        low_tmp[r, :] = normed.astype(low)
        two_rows = normed * gain_ff[...]
        wide[r, :] = two_rows
        cols[6, r, :] = two_rows.astype(low)
        return carry

    over_rows(norm_second)
    share_col(7)
    norm_two[...] = low_tmp[...].T.reshape(blocks, PIECE, tokens)
    stat_two[...] = stat[...].T[:8]
    put_t(3, cols[6].T)
    share_row(3)

    slot_query = take()
    low_tmp[...] = matmul(cols[6], ring[slot_query]).astype(low)
    put_t(4, low_tmp[...].T)
    share_row(4)
    slot_key = take()
    put_t(2, matmul(ring[slot_key], get_t(4)).astype(low))
    share_row(2)

    for i in range(2):
        bank_own[i].wait()
        bank_sib[i].wait_recv()
        bank_far[i].wait_recv()
    acc_t[...] = matmul(banks[0].reshape(width, width), get_t(3)).reshape(blocks, PIECE, tokens)
    acc_t_two[...] = matmul(banks[1].reshape(width, width), get_t(2)).reshape(
        blocks, PIECE, tokens
    )
    score_scale = 1.0 / math.sqrt(width)
    groups = PIECE // adapters

    def grouped(value):
        return value.reshape(groups, adapters, tokens)

    def adapter_rows(p, logits):
        inner = acc_t[p]
        cdf, density = normal_parts(inner)
        act = inner * cdf
        active[p] = act
        bank_slope[p] = (cdf + inner * density).astype(low)
        return logits + grouped(act * acc_t_two[p]).sum(0)

    logits = over_pieces(adapter_rows, jnp.zeros((adapters, tokens), jnp.float32)) * score_scale
    logits = jnp.exp(logits - jnp.max(logits, 0, keepdims=True))
    shares = logits / jnp.sum(logits, 0, keepdims=True)

    def spread(value):
        return jnp.concatenate([value] * groups, 0)

    wide_shares = spread(shares)

    def mixing_rows(p, carry):
        low_tmp_two[pl.ds(pl.multiple_of(p * PIECE, PIECE), PIECE), :] = (
            wide_shares * active[p]
        ).astype(low)
        return carry

    over_pieces(mixing_rows)
    cols[8] = low_tmp_two[...].T
    share_col(9)
    acc[...] = matmul(cols[8], banks[1].reshape(width, width))

    def joined_rows(r, i, carry):
        cols[7, r, :] = (wide[r, :] + acc[r, :]).astype(low)
        return carry

    over_rows(joined_rows)
    share_col(8)
    slot_value = take()
    acc[...] = matmul(cols[7], ring[slot_value])

    def norm_third(r, i, gain_part):
        normed, rstd = norm_rows(wide[r, :] + acc[r, :])
        gain = gain_out[...]
        acc_two[r, :] = normed * gain
        token = lax.broadcasted_iota(jnp.int32, (step_rows, 1), 0) + i * step_rows
        upstream = jnp.where(token < length, cotangent[r, :].astype(jnp.float32), 0.0)
        product = upstream * normed
        gained = upstream * gain
        third = rstd * (
            gained
            - jnp.mean(gained, -1, keepdims=True)
            - normed * jnp.mean(gained * normed, -1, keepdims=True)
        )
        low_tmp[r, :] = third.astype(low)
        return gain_part + product.reshape(step_rows // 8, 8, width).sum(0)

    gain_part = over_rows(norm_third, jnp.zeros((8, width), jnp.float32))
    out_copy = pltpu.make_async_copy(acc_two, output, local_sem.at[2])
    out_copy.start()
    gain_sum[0] = jnp.broadcast_to(jnp.sum(gain_part, 0, keepdims=True), (8, width))
    put_t(0, low_tmp[...].T)
    share_row(0)

    second[...] = matmul(ring[slot_value], get_t(0)).reshape(blocks, PIECE, tokens)
    release(slot_value)

    def mix_rows(p, carry):
        zz, xx, cc = spot(p)
        rows[1, zz, xx, cc] = second[p].astype(low)
        return carry

    over_pieces(mix_rows)
    share_row(1)

    acc_t[...] = matmul(banks[1].reshape(width, width), get_t(1)).reshape(blocks, PIECE, tokens)
    reduce_step(0)

    def share_rows(p, total):
        return total + grouped(acc_t[p] * active[p]).sum(0)

    share_grad = over_pieces(share_rows, jnp.zeros((adapters, tokens), jnp.float32))
    logit_grad = shares * (share_grad - jnp.sum(shares * share_grad, 0, keepdims=True))
    wide_logit = spread(logit_grad * score_scale)

    def adapter_back(p, carry):
        act_grad = acc_t[p] * wide_shares + wide_logit * acc_t_two[p]
        where = pl.ds(pl.multiple_of(p * PIECE, PIECE), PIECE)
        low_tmp_two[where, :] = (wide_logit * active[p]).astype(low)
        bank_slope[p] = (bank_slope[p].astype(jnp.float32) * act_grad).astype(low)
        return carry

    over_pieces(adapter_back)
    cols[9] = low_tmp_two[...].T
    share_col(10)
    cols[10] = bank_slope[...].reshape(width, tokens).T
    share_col(11)
    cols[11] = matmul(cols[9], banks[1].reshape(width, width)).astype(low)
    share_col(12)
    low_tmp[...] = matmul(cols[11], ring[slot_key]).astype(low)
    release(slot_key)
    put_t(5, low_tmp[...].T)
    share_row(5)
    low_tmp[...] = matmul(cols[10], banks[0].reshape(width, width)).astype(low)
    low_tmp_two[...] = low_tmp[...].T
    acc_t[...] = matmul(ring[slot_query], get_t(5)).reshape(blocks, PIECE, tokens)
    release(slot_query)
    reduce_step(1)

    reduce_step(2)

    def norm_back(index, gain, normed_ref, stat_ref, upstream_of, factor):
        gain_col[...] = jnp.broadcast_to(gain[...], (128, width)).T.reshape(blocks, PIECE, 128)

        def gained(p):
            column = gain_col[p]
            return acc_t[p] * jnp.concatenate([column] * (tokens // 128), 1)

        def first_pass(p, carry):
            upstream = upstream_of(p)
            acc_t[p] = upstream
            normed = normed_ref[p].astype(jnp.float32)
            gain_of = jnp.sum(upstream * normed, -1, keepdims=True)
            weighted = gained(p)
            gain_col[p] = jnp.broadcast_to(gain_of, (PIECE, 128))
            acc_t[p] = weighted
            return carry[0] + fold(weighted), carry[1] + fold(weighted * normed)

        zeros = jnp.zeros((8, tokens), jnp.float32)
        plain, tilted = over_pieces(first_pass, (zeros, zeros))
        mean_plain = jnp.sum(plain, 0, keepdims=True) * (1.0 / width)
        mean_tilted = jnp.sum(tilted, 0, keepdims=True) * (1.0 / width)
        rstd = stat_ref[0:1, :]

        def second_pass(p, carry):
            value = rstd * (acc_t[p] - mean_plain - normed_ref[p].astype(jnp.float32) * mean_tilted)
            second[p] = value
            zz, xx, cc = spot(p)
            rows[factor, zz, xx, cc] = value.astype(low)
            return carry

        over_pieces(second_pass)
        gain_sum[0, index : index + 1, :] = gain_col[...].reshape(width, 128).T[:1]

    def upstream_two(p):
        zz, xx, cc = spot(p)
        where = pl.ds(pl.multiple_of(p * PIECE, PIECE), PIECE)
        total = rows[0, zz, xx, cc].astype(jnp.float32) + second[p]
        return total + low_tmp_two[where, :].astype(jnp.float32) + acc_t[p]

    norm_back(1, gain_ff, norm_two, stat_two, upstream_two, 6)
    share_row(6)
    reduce_step(3)
    reduce_step(4)

    for k in range(4):
        slot = take()
        acc_t_two[...] = matmul(ring[slot], get_t(6)).reshape(blocks, PIECE, tokens)
        release(slot)

        def slope_rows(p, carry):
            value = acc_t_two[p] * slope[k * blocks + p].astype(jnp.float32)
            rows_ff[k, p // 8, (p % 8) // 2, p % 2] = value.astype(low)
            return carry

        over_pieces(slope_rows)
        slot = take()
        value = matmul(ring[slot], rows_ff[k].reshape(width, tokens))
        value = value.reshape(blocks, PIECE, tokens)
        release(slot)
        acc_t[...] = value if k == 0 else acc_t[...] + value
        reduce_step(5 + k)
    for index in range(8, 12):
        share_row(index)

    def upstream_one(p):
        return second[p] + acc_t[p]

    norm_back(0, gain_attn, norm_one, stat_one, upstream_one, 7)
    share_row(7)
    gain_copy = send(gain_sum.at[0], gain_from.at[0], gain_send.at[0], gain_recv.at[0], sibling)
    slot = take()
    low_tmp_two[...] = matmul(ring[slot], get_t(7)).astype(low)
    release(slot)
    reduce_step(9)

    heads_step = 3
    step_pieces = heads_step * size // PIECE

    def head_backward(group, carry):
        grads = [[], [], []]
        for i in range(heads_step):
            head = group * heads_step + i
            query, key, value = [qkv_t[head_rows(k, head), :] for k in range(3)]
            upstream = low_tmp_two[pl.ds(pl.multiple_of(head * size, size), size), :]
            share = probs[head]
            share_wide = share.astype(jnp.float32)
            prob_grad = matmul_tn(value, upstream)
            delta = jnp.sum(share_wide * prob_grad, 0, keepdims=True)
            score_grad = (share_wide * (prob_grad - delta)).astype(low)
            grads[0].append((matmul(key, score_grad) * 0.125).astype(low))
            grads[1].append(matmul_t(query, score_grad).astype(low))
            grads[2].append(matmul_t(upstream, share).astype(low))
        for k in range(3):
            stacked = jnp.concatenate(grads[k], 0).reshape(step_pieces, PIECE, tokens)
            for i in range(step_pieces):
                p = k * blocks + group * step_pieces + i
                rows_qkv[p // 12, (p // 6) % 2, (p % 6) // 2, p % 2] = stacked[i]
        return carry

    lax.fori_loop(0, heads // heads_step, head_backward, 0)
    for index in range(12, 15):
        share_row(index)
    for step in range(10, 14):
        reduce_step(step)
    gain_copy.wait_recv()
    gain_sum[1] = gain_sum[0] + gain_from[0]
    gain_copy = send(gain_sum.at[1], gain_from.at[1], gain_send.at[1], gain_recv.at[1], x_mate)
    reduce_step(14)
    reduce_step(15)
    reduce_step(16)
    for k in range(3):
        slot = take()
        block = rows_qkv[...].reshape(3 * blocks, PIECE, tokens)[k * blocks : (k + 1) * blocks]
        value = matmul(ring[slot], block.reshape(width, tokens)).reshape(blocks, PIECE, tokens)
        release(slot)
        second[...] = second[...] + value
    acc[...] = second[...].reshape(width, tokens).T
    in_copy = pltpu.make_async_copy(acc, grad_in, local_sem.at[3])
    in_copy.start()

    for step in range(units, units + LAG_FOUR):
        reduce_step(step)
        if step == units:
            gain_copy.wait_recv()
            gain_sum[2] = gain_sum[1] + gain_from[1]
            gain_copy = send(
                gain_sum.at[2], gain_from.at[2], gain_send.at[2], gain_recv.at[2], y_mate
            )
        if step == units + 2:
            gain_copy.wait_recv()
            gain_sum[3] = gain_sum[2] + gain_from[2]
            gain_copies = [
                send(
                    gain_sum.at[3],
                    gain_from.at[3 + k],
                    gain_send.at[3 + k],
                    gain_recv.at[3 + k],
                    z_mates[k],
                )
                for k in range(3)
            ]
        if step == units + 5:
            total = gain_sum[3]
            for k in range(3):
                gain_copies[k].wait_recv()
                total += gain_from[3 + k]
            gain_sums[...] = total
    for unit in range(units):
        last[unit].wait_recv()
    for copy in started:
        copy.wait_send()
    out_copy.wait()
    in_copy.wait()


def run_layer(heads, adapters, arrays):
    hidden = arrays[0]
    tokens, width = hidden.shape
    low, wide = jnp.bfloat16, jnp.float32
    blocks = width // PIECE
    units = len(UNITS)
    dma = pltpu.SemaphoreType.DMA
    vmem = pl.BlockSpec(memory_space=pltpu.VMEM)
    smem = pl.BlockSpec(memory_space=pltpu.SMEM)
    far = pl.BlockSpec(memory_space=pl.ANY)
    half_width = width // 2
    pair = lambda shape: [dma(shape), dma(shape)]
    return pl.pallas_call(
        functools.partial(layer_kernel, heads, adapters),
        out_shape=(
            jax.ShapeDtypeStruct((tokens, width), wide),
            jax.ShapeDtypeStruct((tokens, width), wide),
            jax.ShapeDtypeStruct((units, 2, PIECE, half_width), low),
            jax.ShapeDtypeStruct((8, width), wide),
        ),
        in_specs=[
            vmem, smem, vmem, far, far, vmem, far, far, vmem, far, far, far, far, far, vmem,
        ],
        out_specs=[far, far, vmem, vmem],
        scratch_shapes=[
            pltpu.VMEM((8, 4, 2, 2, PIECE, tokens), low),
            pltpu.VMEM((4, 2, 4, 2, PIECE, tokens), low),
            pltpu.VMEM((4, 2, 3, 2, PIECE, tokens), low),
            pltpu.VMEM((15, 4, 2, PIECE, tokens), low),
            pltpu.VMEM((12, tokens, width), low),
            pltpu.VMEM((13, tokens, width), low),
            pltpu.VMEM((SLOTS, width, width), low),
            pltpu.VMEM((2, 4, width // 4, width), low),
            pltpu.VMEM((tokens, width), wide),
            pltpu.VMEM((tokens, width), wide),
            pltpu.VMEM((tokens, width), wide),
            pltpu.VMEM((blocks, PIECE, tokens), wide),
            pltpu.VMEM((blocks, PIECE, tokens), wide),
            pltpu.VMEM((blocks, PIECE, tokens), wide),
            pltpu.VMEM((blocks, PIECE, tokens), low),
            pltpu.VMEM((blocks, PIECE, tokens), wide),
            pltpu.VMEM((blocks, PIECE, tokens), low),
            pltpu.VMEM((blocks, PIECE, tokens), low),
            pltpu.VMEM((4 * blocks, PIECE, tokens), low),
            pltpu.VMEM((3 * width, tokens), low),
            pltpu.VMEM((heads, tokens, tokens), low),
            pltpu.VMEM((tokens, width), low),
            pltpu.VMEM((width, tokens), low),
            pltpu.VMEM((tokens, 128), wide),
            pltpu.VMEM((8, tokens), wide),
            pltpu.VMEM((8, tokens), wide),
            pltpu.VMEM((blocks, PIECE, 128), wide),
            pltpu.VMEM((units, 2, 2, 4, PIECE, half_width), low),
            pltpu.VMEM((units, 2, 4, PIECE, half_width), low),
            pltpu.VMEM((units, 4, PIECE, half_width), low),
            pltpu.VMEM((units, 3, PIECE, half_width), low),
            pltpu.VMEM((4, 8, width), wide),
            pltpu.VMEM((6, 8, width), wide),
            dma((SLOTS,)),
            dma((4,)),
        ]
        + pair((2, 3))
        + pair((15,))
        + pair((13,))
        + pair((units,))
        + pair((units,))
        + pair((units, 3))
        + pair((units,))
        + pair((6,)),
        compiler_params=pltpu.CompilerParams(
            collective_id=0, has_side_effects=True, vmem_limit_bytes=63 * 2**20
        ),
    )(*arrays)


def finish_kernel(
    sums,
    gain_sums,
    out_qkv,
    out_proj,
    out_gain_attn,
    out_ff_in,
    out_ff_out,
    out_gain_ff,
    out_query,
    out_key,
    out_value,
    out_down,
    out_up,
    out_gain_out,
    turned,
):
    ad = lax.axis_index("ad")
    core = lax.axis_index("bn") % 2
    width = sums.shape[3]
    own = pl.ds(pl.multiple_of(core * (width // 2), width // 2), width // 2)

    def columns(out, slot, first, count):
        value = sums[first : first + count].reshape(count * 2 * PIECE, width)
        extent = pl.ds(0, count * 2 * PIECE)
        turned[slot, :, extent] = value.astype(jnp.float32).T
        out[...] = turned[slot, own, extent]

    columns(out_value, 0, 0, 1)
    columns(out_up, 1, 1, 1)
    columns(out_down, 2, 2, 1)
    columns(out_key, 0, 3, 1)
    columns(out_query, 1, 4, 1)
    columns(out_ff_in, 2, 9, 4)
    columns(out_proj, 0, 13, 1)
    columns(out_qkv, 1, 14, 3)
    for i in range(2):
        value = sums[5 + 2 * core + i].reshape(2 * PIECE, width)
        out_ff_out[pl.ds(i * width, width), :] = value.astype(jnp.float32).T
    total = gain_sums.shape[1]
    piece = out_gain_attn.shape[1]
    rolled = pltpu.roll(gain_sums[...], lax.rem(total - ad * piece, total), 1)[:, :piece]
    out_gain_attn[...] = rolled[0:1]
    out_gain_ff[...] = rolled[1:2]
    out_gain_out[...] = rolled[2:3]


def finish(sums, gain_sums, width):
    quarter, eighth = width // 4, width // 8
    shapes = [
        (quarter, 3 * eighth),
        (quarter, eighth),
        (1, eighth),
        (quarter, 4 * eighth),
        (4 * quarter, eighth),
        (1, eighth),
    ]
    shapes += [(quarter, eighth)] * 5 + [(1, eighth)]
    return pl.pallas_call(
        finish_kernel,
        out_shape=tuple(jax.ShapeDtypeStruct(shape, jnp.float32) for shape in shapes),
        in_specs=[pl.BlockSpec(memory_space=pltpu.VMEM)] * 2,
        out_specs=[pl.BlockSpec(memory_space=pltpu.VMEM)] * 12,
        scratch_shapes=[pltpu.VMEM((3, width // 2, 4 * eighth), jnp.float32)],
        compiler_params=pltpu.CompilerParams(vmem_limit_bytes=32 * 2**20),
    )(sums, gain_sums)


def fast_local(*arrays):
    arrays = list(arrays)
    width = arrays[0].shape[1]
    adapters = arrays[12].shape[1]
    for i in (5, 8, 14):
        arrays[i] = arrays[i].reshape(1, width)
    bank_shape = arrays[12].shape[:2] + (-1,)
    for i in (12, 13):
        arrays[i] = arrays[i].reshape(-1, width)
    output, grad_in, sums, gain_sums = run_layer(H, adapters, arrays)
    grads = list(finish(sums, gain_sums, width))
    for i in (2, 5, 11):
        grads[i] = grads[i].reshape(-1)
    for i in (9, 10):
        grads[i] = grads[i].reshape(bank_shape)
    return (output, grad_in, *grads)


def local(
    hidden_in,
    lengths,
    cotangent,
    w_qkv,
    w_out,
    gain_attn,
    w_ff_in,
    w_ff_out,
    gain_ff,
    join_query,
    join_key,
    join_value,
    adapt_down,
    adapt_up,
    gain_out,
):
    seq_count = lengths.shape[0]
    tok_rows, model_width = hidden_in.shape
    slot_len = tok_rows // seq_count
    head_count = H
    head_size = model_width // head_count
    score_scale = 1.0 / math.sqrt(head_size)
    adapters = adapt_down.shape[1]
    down_flat = lax.all_gather(adapt_down.reshape(-1, model_width), "bn", axis=0, tiled=True)
    up_flat = lax.all_gather(adapt_up.reshape(-1, model_width), "bn", axis=0, tiled=True)
    valid = lax.broadcasted_iota(jnp.int32, (seq_count, slot_len), 1) < lengths[:, None]
    row_ok = valid.reshape(tok_rows, 1).astype(jnp.float32)
    tokens_wide = hidden_in.astype(jnp.float32)
    qkv = matmul(hidden_in, w_qkv).astype(jnp.bfloat16)
    queries = qkv[:, :model_width].reshape(seq_count, slot_len, head_count, head_size)
    key_rows = qkv[:, model_width : 2 * model_width].reshape(
        seq_count, slot_len, head_count, head_size
    )
    values = qkv[:, 2 * model_width :].reshape(seq_count, slot_len, head_count, head_size)

    def attend_scores():
        raw_scores = (
            jnp.einsum("sqhe,skhe->shqk", queries, key_rows, preferred_element_type=jnp.float32)
            * score_scale
        )
        return jnp.where(valid[:, None, None, :], raw_scores, masked_value)

    scores = attend_scores()
    row_max = jnp.max(scores, -1, keepdims=True)
    log_total = row_max + jnp.log(jnp.sum(jnp.exp(scores - row_max), -1, keepdims=True))
    probs = jnp.exp(scores - log_total).astype(jnp.bfloat16)
    context = (
        jnp.einsum("shqk,skhe->sqhe", probs, values, preferred_element_type=jnp.float32)
        .reshape(tok_rows, model_width)
        .astype(jnp.bfloat16)
    )
    attn_out = matmul(context, w_out)
    hidden_one, norm_one_back = jax.vjp(layer_norm, tokens_wide + attn_out, gain_attn)
    hidden_one_low = hidden_one.astype(jnp.bfloat16)
    ff_pre = matmul(hidden_one_low, w_ff_in)
    ff_act, gelu_ff_back = jax.vjp(gelu_exact, ff_pre)
    ff_low = ff_act.astype(jnp.bfloat16)
    ff_out = matmul(ff_low, w_ff_out)
    hidden_two, norm_two_back = jax.vjp(layer_norm, hidden_one + ff_out, gain_ff)
    hidden_low = hidden_two.astype(jnp.bfloat16)
    query_join = matmul(hidden_low, join_query).astype(jnp.bfloat16)
    probe = matmul_t(query_join, join_key).astype(jnp.bfloat16)
    mixing, kept_state = adapter_forward(hidden_low, probe, down_flat, up_flat, adapters)
    joined_in = (hidden_two + matmul(mixing, up_flat)).astype(jnp.bfloat16)
    joined = matmul(joined_in, join_value)
    output, norm_out_back = jax.vjp(layer_norm, hidden_two + joined, gain_out)
    out_grad = cotangent.astype(jnp.float32) * row_ok
    sum_three, gain_out_grad = norm_out_back(out_grad)
    joined_grad = sum_three.astype(jnp.bfloat16)
    into_joined = matmul_t(joined_grad, join_value)
    mix_grad = into_joined.astype(jnp.bfloat16)
    inner_grad, weigh_grad = adapter_backward(kept_state, up_flat, mix_grad, adapters)
    hidden_back = matmul(inner_grad, down_flat)
    probe_grad = matmul(weigh_grad, up_flat).astype(jnp.bfloat16)
    query_in = matmul(probe_grad, join_key).astype(jnp.bfloat16)
    grad_two = sum_three + into_joined + hidden_back + matmul_t(query_in, join_query)
    sum_two, gain_ff_grad = norm_two_back(grad_two)
    ff_out_grad = sum_two.astype(jnp.bfloat16)
    ff_pre_grad = gelu_ff_back(matmul_t(ff_out_grad, w_ff_out))[0].astype(jnp.bfloat16)
    grad_one = sum_two + matmul_t(ff_pre_grad, w_ff_in)
    sum_one, gain_attn_grad = norm_one_back(grad_one)
    attn_grad = sum_one.astype(jnp.bfloat16)
    context_grad = (
        matmul_t(attn_grad, w_out)
        .astype(jnp.bfloat16)
        .reshape(seq_count, slot_len, head_count, head_size)
    )
    probs_wide = jnp.exp(attend_scores() - log_total)
    prob_grad = jnp.einsum(
        "sqhe,skhe->shqk", context_grad, values, preferred_element_type=jnp.float32
    )
    row_delta = jnp.sum(probs_wide * prob_grad, -1, keepdims=True)
    score_grad = (probs_wide * (prob_grad - row_delta)).astype(jnp.bfloat16)
    query_back = (
        jnp.einsum("shqk,skhe->sqhe", score_grad, key_rows, preferred_element_type=jnp.float32)
        * score_scale
    )
    key_back = (
        jnp.einsum("shqk,sqhe->skhe", score_grad, queries, preferred_element_type=jnp.float32)
        * score_scale
    )
    value_back = jnp.einsum(
        "shqk,sqhe->skhe", probs, context_grad, preferred_element_type=jnp.float32
    )
    qkv_grad = jnp.concatenate(
        [
            query_back.reshape(tok_rows, model_width),
            key_back.reshape(tok_rows, model_width),
            value_back.reshape(tok_rows, model_width),
        ],
        1,
    ).astype(jnp.bfloat16)
    grad_in = sum_one + matmul_t(qkv_grad, w_qkv)
    def shared_sum(gradient):
        columns = lax.psum_scatter(gradient, "ad", scatter_dimension=1, tiled=True)
        return lax.psum_scatter(
            columns.astype(jnp.bfloat16), "bn", scatter_dimension=0, tiled=True
        ).astype(jnp.float32)

    gains = lax.psum(
        lax.psum_scatter(
            jnp.stack([gain_attn_grad, gain_ff_grad, gain_out_grad]),
            "ad",
            scatter_dimension=1,
            tiled=True,
        ),
        "bn",
    )
    down_grad = shared_sum(matmul_tn(inner_grad, hidden_low))
    up_grad = shared_sum(matmul_tn(mixing, mix_grad) + matmul_tn(weigh_grad, probe))
    bank = adapt_down.shape[:2] + (-1,)
    return (
        output,
        grad_in,
        shared_sum(matmul_tn(hidden_in, qkv_grad)),
        shared_sum(matmul_tn(context, attn_grad)),
        gains[0],
        shared_sum(matmul_tn(hidden_one_low, ff_pre_grad)),
        shared_sum(matmul_tn(ff_low, ff_out_grad)),
        gains[1],
        shared_sum(matmul_tn(hidden_low, query_in)),
        shared_sum(matmul_tn(probe_grad, query_join)),
        shared_sum(matmul_tn(joined_in, joined_grad)),
        down_grad.reshape(bank),
        up_grad.reshape(bank),
        gains[2],
    )


def solution(mesh):
    placed = (
        P(("ad", "bn"), None),
        P(("ad", "bn")),
        P(("ad", "bn"), None),
        P(),
        P(),
        P(),
        P(),
        P(),
        P(),
        P(),
        P(),
        P(),
        P("bn", None, None),
        P("bn", None, None),
        P(),
    )
    sizes = (mesh.shape["ad"], mesh.shape["bn"])
    return jax.shard_map(
        fast_local if sizes == (8, 4) else local,
        mesh=mesh,
        in_specs=placed,
        out_specs=(
            P(("ad", "bn"), None),
            P(("ad", "bn"), None),
            P("bn", "ad"),
            P("bn", "ad"),
            P("ad"),
            P("bn", "ad"),
            P("bn", "ad"),
            P("ad"),
            P("bn", "ad"),
            P("bn", "ad"),
            P("bn", "ad"),
            P("bn", None, "ad"),
            P("bn", None, "ad"),
            P("ad"),
        ),
        check_vma=False,
    )
```

profile of v0, /device:TPU:0, one launch (start us, length us, event | category | flops | bytes accessed | tf_op | source)
XLA Modules:
  0.0 148.4 jit_solution(14867376939821181895)
XLA Ops:
  1.3 1.3 reshape.58.gain_attn
  2.6 1.3 reshape.59.gain_ff
  3.8 1.3 reshape.62.gain_out
  5.1 137.0 %shard_map.254 = (f32[256,768]{1,0:T(8,128)}, f32[256,768]{1,0:T(8,128)}, bf16[17,2,48,384]{3,2,1,0:T(8,128)(2,1)}, f32[8,768]{1,0:T(8,128)}) custom-call(bf16[256,768]{1,0:T(8,128)(2,1)} %hidden.1, s32[1]{0:T(128)S(6)} %copy.32.lengths, bf16[256,768]{1,0:T(8,128)(2,1)} %cotangent.1, bf16[768,2304]{1,0:T(8,128)(2,1)} %w_qkv.1, bf16[768,768]{1,0:T(8,128)(2,1)} %w_out.1, ...), custom_call_target="tpu_custom_call" | custom-call | tf_op jit(solution)/shard_map/pallas_call | solution.py:847
  142.1 0.0 copy-start
  142.1 1.3 copy-done
  143.4 0.0 copy-start.1
  143.4 0.7 copy-done.1
  144.1 0.0 copy-start.3
  144.1 1.6 %shard_map.255 = (f32[192,288]{1,0:T(8,128)}, f32[192,96]{1,0:T(8,128)}, f32[1,96]{1,0:T(1,128)}, f32[192,384]{1,0:T(8,128)}, f32[768,96]{1,0:T(8,128)S(1)}, /*i...) custom-call(bf16[17,2,48,384]{3,2,1,0:T(8,128)(2,1)S(1)} %copy-done,, ...), custom_call_target="tpu_custom_call" | custom-call | tf_op jit(solution)/shard_map/pallas_call | solution.py:968
  145.8 0.0 copy-start.2
  145.8 0.9 copy.29
  146.7 0.0 copy-done.3
  146.7 0.9 copy.33
  147.5 0.0 copy-done.2
  147.5 0.9 copy.34
Async XLA Ops:
  142.1 1.3 copy-start
  143.4 0.7 copy-start.1
  144.1 2.5 %copy-start.3 = (f32[256,768]{1,0:T(8,128)S(1)}, f32[256,768]{1,0:T(8,128)}, u32[]{:S(2)}) copy-start(f32[256,768]{1,0:T(8,128)} %get-tuple-element.74) | copy-start | bytes 2359300
  145.8 1.8 %copy-start.2 = (f32[256,768]{1,0:T(8,128)S(1)}, f32[256,768]{1,0:T(8,128)}, u32[]{:S(2)}) copy-start(f32[256,768]{1,0:T(8,128)} %get-tuple-element.75) | copy-start | bytes 2359300
where the time goes:
time: 149 us; the launch traced here: 148 us
  Pallas kernels  139 us (93%)
  local copies, waits for them, and re-layouts  8.47 us (6%)
    pallas_call x1, Pallas kernels, run_layer(): pl.pallas_call(functools.partial(layer_kernel, heads, adapters), out_shap...  137 us
    unnamed x11, local copies, waits for them, and re-layouts  4.67 us
    reshape x3, local copies, waits for them, and re-layouts, fast_local(): arrays[i] = arrays[i].reshape(1, width)  3.8 us

commit v1 on v0

--- a/solution.py
+++ b/solution.py
@@ -81,9 +81,6 @@
 
 PIECE = 48
 SLOTS = 5
-LAG_TWO = 4
-LAG_THREE = 6
-LAG_FOUR = 8
 UNITS = (
     ((0, 8),),
     ((1, 9), (2, 10)),
@@ -104,6 +101,32 @@
     ((14, 0),),
 )
 
+
+ORDERS = (
+    ("y", "x", "l", "h"),
+    ("l", "y", "x", "h"),
+    ("x", "l", "h", "y"),
+    ("y", "x", "l", "h"),
+    ("y", "l", "x", "h"),
+    ("y", "l", "x", "h"),
+    ("l", "x", "y", "h"),
+    ("x", "l", "h", "y"),
+    ("y", "x", "l", "h"),
+    ("x", "l", "h", "y"),
+    ("x", "l", "y", "h"),
+    ("l", "x", "h", "y"),
+    ("y", "x", "l", "h"),
+    ("x", "y", "l", "h"),
+    ("y", "x", "l", "h"),
+    ("y", "l", "x", "h"),
+    ("x", "y", "l", "h"),
+)
+SEQUENCE = (
+    -1, -1, 0, -1, 2, 1, -1, 3, -1, 7, 6, 8, -1, -1, -1, 0, -1, 2, 9, 11, 4, -1, 13, 5,
+    -1, 2, 16, 0, 15, 7, 9, 10, 14, 0, 4, 7, 5, 12, 0, 3, 9, 15, 4, 11, 10, 5, 2, 7, 3,
+    8, 9, 16, 4, 15, 13, 11, 14, 2, 5, 3, 7, 4, 9, 10, 6, 1, 8, 16, 5, 15, 12, 11, 3, 8,
+    13, 16, 14, 15, 10, 8, 13, 6, 16, 1, 11, 14, 10, 12, 6, 13, 1, 14, 12, 6, 1, 12,
+)
 
 def flip(index, bit):
     return index + bit - 2 * bit * ((index // bit) % 2)
@@ -168,6 +191,7 @@
     recv_one,
     recv_two,
     recv_three,
+    recv_four,
     gain_sum,
     gain_from,
     ring_sem,
@@ -178,12 +202,8 @@
     row_recv,
     col_send,
     col_recv,
-    one_send,
-    one_recv,
-    two_send,
-    two_recv,
-    three_send,
-    three_recv,
+    stage_send,
+    stage_recv,
     last_send,
     last_recv,
     gain_send,
@@ -192,6 +212,9 @@
     low = jnp.bfloat16
     tokens, width = hidden.shape
     half_width = width // 2
+    gain_attn, gain_ff, gain_out = [
+        gain[...].reshape(1, width) for gain in (gain_attn, gain_ff, gain_out)
+    ]
     blocks = rows.shape[1] * rows.shape[2] * rows.shape[3]
     ad = lax.axis_index("ad")
     bn = lax.axis_index("bn")
@@ -200,9 +223,9 @@
     sibling = (ad, flip(bn, 1))
     x_mate = (flip(ad, 1), bn)
     y_mate = (ad, flip(bn, 2))
-    z_index = [flip(z, 1), flip(z, 2), flip(flip(z, 1), 2)]
-    z_mates = [(zz * 2 + x, bn) for zz in z_index]
-    other_core, other_x, other_y = 1 - core, 1 - x, 1 - y
+    own = {"y": y, "x": x, "h": z // 2, "l": z % 2}
+    mates = {"y": y_mate, "x": x_mate, "h": (flip(ad, 4), bn), "l": (flip(ad, 2), bn)}
+    other_core = 1 - core
 
     loads = [(w_qkv.at[:, pl.ds(k * width, width)]) for k in range(3)] + [w_out]
     for k in range(4):
@@ -241,9 +264,8 @@
         bank_own[i].start()
 
     barrier = pltpu.get_barrier_semaphore()
-    for mate in [sibling, x_mate, y_mate] + z_mates:
+    for mate in [sibling, *mates.values()]:
         pl.semaphore_signal(barrier, inc=1, device_id=mate, device_id_type=MESH)
-    pl.semaphore_wait(barrier, 6)
 
     started = []
 
@@ -260,16 +282,6 @@
         started.append(copy)
         return copy
 
-    bank_sib, bank_y, bank_far = [], [], []
-    for i, bank in enumerate((adapt_down, adapt_up)):
-        bank_y.append(
-            send(bank, banks.at[i, bn], bank_send.at[i, 1], bank_recv.at[i, 1], y_mate)
-        )
-    for i, bank in enumerate((adapt_down, adapt_up)):
-        bank_sib.append(
-            send(bank, banks.at[i, bn], bank_send.at[i, 0], bank_recv.at[i, 0], sibling)
-        )
-
     def row_views(index):
         if index < 8:
             return rows.at[index]
@@ -310,7 +322,9 @@
             sibling,
         )
 
-    one, two, three, last = {}, {}, {}, {}
+    axes = ("y", "x", "h", "l")
+    recvs = (recv_one, recv_two, recv_three, recv_four)
+    copies, last = {}, {}
     units = len(UNITS)
 
     def half(unit, side):
@@ -327,78 +341,55 @@
                 rows_sib[left, :, side].reshape(4 * PIECE, tokens), cols_sib[right]
             )
             total = term if total is None else total + term
-        total = total.astype(low).reshape(4, PIECE, width)
-        part[unit, 0, side] = total[:, :, :half_width]
-        part[unit, 1, side] = total[:, :, half_width:]
-
-    def stage_one(unit):
-        if unit % 2 == 0:
-            half(unit, other_x)
-            one[unit] = send(
-                part.at[unit, :, other_x],
-                recv_one.at[unit],
-                one_send.at[unit],
-                one_recv.at[unit],
-                x_mate,
-            )
+        total = total.astype(low).reshape(2, 2, PIECE, width)
+        part[unit, 0, side] = total[..., :half_width]
+        part[unit, 1, side] = total[..., half_width:]
+
+    def place(done, axis, index):
+        fixed = {name: own[name] for name in done}
+        fixed[axis] = index
+        left = [name for name in axes if name not in done]
+        inside = tuple(index if name == axis else slice(None) for name in left)
+        return tuple(fixed.get(name, slice(None)) for name in axes), inside
+
+    def push(unit, stage):
+        order = ORDERS[unit]
+        axis = order[stage]
+        where, _ = place(order[:stage], axis, 1 - own[axis])
+        copies[unit, stage] = send(
+            part.at[(unit, *where)],
+            recvs[stage].at[unit],
+            stage_send.at[stage, unit],
+            stage_recv.at[stage, unit],
+            mates[axis],
+        )
+
+    def start(unit):
+        if ORDERS[unit][0] == "x":
+            half(unit, 1 - x)
+            push(unit, 0)
             half(unit, x)
         else:
             half(unit, 0)
             half(unit, 1)
-            one[unit] = send(
-                part.at[unit, other_y],
-                recv_one.at[unit],
-                one_send.at[unit],
-                one_recv.at[unit],
-                y_mate,
-            )
-
-    def add_low(left, right):
-        return (left.astype(jnp.float32) + right.astype(jnp.float32)).astype(low)
-
-    def stage_two(unit):
-        one[unit].wait_recv()
-        if unit % 2 == 0:
-            part[unit, other_y, x] = add_low(part[unit, other_y, x], recv_one[unit, other_y])
-            two[unit] = send(
-                part.at[unit, other_y, x],
-                recv_two.at[unit],
-                two_send.at[unit],
-                two_recv.at[unit],
-                y_mate,
-            )
-            part[unit, y, x] = add_low(part[unit, y, x], recv_one[unit, y])
-        else:
-            part[unit, y, other_x] = add_low(part[unit, y, other_x], recv_one[unit, other_x])
-            two[unit] = send(
-                part.at[unit, y, other_x],
-                recv_two.at[unit],
-                two_send.at[unit],
-                two_recv.at[unit],
-                x_mate,
-            )
-            part[unit, y, x] = add_low(part[unit, y, x], recv_one[unit, x])
-
-    def stage_three(unit):
-        two[unit].wait_recv()
-        part[unit, y, x] = add_low(part[unit, y, x], recv_two[unit])
-        three[unit] = [
-            send(
-                part.at[unit, y, x, z_index[k]],
-                recv_three.at[unit, k],
-                three_send.at[unit, k],
-                three_recv.at[unit, k],
-                z_mates[k],
-            )
-            for k in range(3)
-        ]
-
-    def stage_four(unit):
-        total = part[unit, y, x, z].astype(jnp.float32)
-        for k in range(3):
-            three[unit][k].wait_recv()
-            total += recv_three[unit, k].astype(jnp.float32)
-        sums[unit, core] = total.astype(low)
+            push(unit, 0)
+
+    def add(unit, stage, axis, index):
+        where, inside = place(ORDERS[unit][: stage + 1], axis, index)
+        mine = part[(unit, *where)].astype(jnp.float32)
+        part[(unit, *where)] = (mine + recvs[stage][(unit, *inside)].astype(jnp.float32)).astype(low)
+
+    def advance(unit, stage):
+        copies[unit, stage].wait_recv()
+        axis = ORDERS[unit][stage + 1]
+        add(unit, stage, axis, 1 - own[axis])
+        push(unit, stage + 1)
+        add(unit, stage, axis, own[axis])
+
+    def close(unit):
+        copies[unit, 3].wait_recv()
+        total = part[(unit, *(own[name] for name in axes))].astype(jnp.float32)
+        sums[unit, core] = (total + recv_four[unit].astype(jnp.float32)).astype(low)
         last[unit] = send(
             sums.at[unit, core],
             sums.at[unit, core],
@@ -407,27 +398,15 @@
             sibling,
         )
 
-    def reduce_step(step):
-        if step < units:
-            stage_one(step)
-        if 0 <= step - LAG_TWO < units:
-            stage_two(step - LAG_TWO)
-        if 0 <= step - LAG_THREE < units:
-            stage_three(step - LAG_THREE)
-        if 0 <= step - LAG_FOUR < units:
-            stage_four(step - LAG_FOUR)
-
-    step_rows = 32
-    row_steps = tokens // step_rows
+    step_rows = tokens
 
     def over_rows(body, init=0):
-        def step(i, carry):
-            return body(pl.ds(pl.multiple_of(i * step_rows, step_rows), step_rows), i, carry)
-
-        return lax.fori_loop(0, row_steps, step, init)
+        return body(slice(None), 0, init)
 
     def over_pieces(body, init=0):
-        return lax.fori_loop(0, blocks, body, init)
+        for p in range(blocks):
+            init = body(p, init)
+        return init
 
     def spot(p):
         return p // 4, (p // 2) % 2, p % 2
@@ -441,7 +420,6 @@
     def fold(value):
         return value.reshape(PIECE // 8, 8, tokens).sum(0)
 
-    share_col(0)
     length = lengths[0]
     for k in range(3):
         slot = take()
@@ -450,6 +428,17 @@
         if k == 0:
             value = value * 0.125
         qkv_t[pl.ds(k * width, width), :] = value.astype(low).T
+    pl.semaphore_wait(barrier, 1 + len(mates))
+    bank_sib, bank_y, bank_far = [], [], []
+    for i, bank in enumerate((adapt_down, adapt_up)):
+        bank_y.append(
+            send(bank, banks.at[i, bn], bank_send.at[i, 1], bank_recv.at[i, 1], y_mate)
+        )
+    for i, bank in enumerate((adapt_down, adapt_up)):
+        bank_sib.append(
+            send(bank, banks.at[i, bn], bank_send.at[i, 0], bank_recv.at[i, 0], sibling)
+        )
+    share_col(0)
     size = width // heads
 
     def head_rows(k, head):
@@ -467,7 +456,7 @@
         low_tmp_two[pl.ds(pl.multiple_of(head * size, size), size), :] = context.astype(low)
         return carry
 
-    lax.fori_loop(0, heads, head_forward, 0)
+    lax.fori_loop(0, heads, head_forward, 0, unroll=3)
     cols[0] = low_tmp_two[...].T
     share_col(1)
     slot = take()
@@ -483,7 +472,7 @@
         normed, rstd = norm_rows(hidden[r, :].astype(jnp.float32) + acc[r, :])
         stat[r, :] = jnp.broadcast_to(rstd, (step_rows, 128))
         low_tmp[r, :] = normed.astype(low)
-        one_rows = normed * gain_attn[...]
+        one_rows = normed * gain_attn
         wide[r, :] = one_rows
         cols[1, r, :] = one_rows.astype(low)
         return carry
@@ -536,7 +525,7 @@
         normed, rstd = norm_rows(wide[r, :] + acc_two[r, :])
         stat[r, :] = jnp.broadcast_to(rstd, (step_rows, 128))
         low_tmp[r, :] = normed.astype(low)
-        two_rows = normed * gain_ff[...]
+        two_rows = normed * gain_ff
         wide[r, :] = two_rows
         cols[6, r, :] = two_rows.astype(low)
         return carry
@@ -588,7 +577,7 @@
     wide_shares = spread(shares)
 
     def mixing_rows(p, carry):
-        low_tmp_two[pl.ds(pl.multiple_of(p * PIECE, PIECE), PIECE), :] = (
+        low_tmp_two[pl.ds(p * PIECE, PIECE), :] = (
             wide_shares * active[p]
         ).astype(low)
         return carry
@@ -609,7 +598,7 @@
 
     def norm_third(r, i, gain_part):
         normed, rstd = norm_rows(wide[r, :] + acc[r, :])
-        gain = gain_out[...]
+        gain = gain_out
         acc_two[r, :] = normed * gain
         token = lax.broadcasted_iota(jnp.int32, (step_rows, 1), 0) + i * step_rows
         upstream = jnp.where(token < length, cotangent[r, :].astype(jnp.float32), 0.0)
@@ -630,55 +619,56 @@
     put_t(0, low_tmp[...].T)
     share_row(0)
 
-    second[...] = matmul(ring[slot_value], get_t(0)).reshape(blocks, PIECE, tokens)
-    release(slot_value)
-
-    def mix_rows(p, carry):
-        zz, xx, cc = spot(p)
-        rows[1, zz, xx, cc] = second[p].astype(low)
-        return carry
-
-    over_pieces(mix_rows)
-    share_row(1)
-
-    acc_t[...] = matmul(banks[1].reshape(width, width), get_t(1)).reshape(blocks, PIECE, tokens)
-    reduce_step(0)
-
-    def share_rows(p, total):
-        return total + grouped(acc_t[p] * active[p]).sum(0)
-
-    share_grad = over_pieces(share_rows, jnp.zeros((adapters, tokens), jnp.float32))
-    logit_grad = shares * (share_grad - jnp.sum(shares * share_grad, 0, keepdims=True))
-    wide_logit = spread(logit_grad * score_scale)
-
-    def adapter_back(p, carry):
-        act_grad = acc_t[p] * wide_shares + wide_logit * acc_t_two[p]
-        where = pl.ds(pl.multiple_of(p * PIECE, PIECE), PIECE)
-        low_tmp_two[where, :] = (wide_logit * active[p]).astype(low)
-        bank_slope[p] = (bank_slope[p].astype(jnp.float32) * act_grad).astype(low)
-        return carry
-
-    over_pieces(adapter_back)
-    cols[9] = low_tmp_two[...].T
-    share_col(10)
-    cols[10] = bank_slope[...].reshape(width, tokens).T
-    share_col(11)
-    cols[11] = matmul(cols[9], banks[1].reshape(width, width)).astype(low)
-    share_col(12)
-    low_tmp[...] = matmul(cols[11], ring[slot_key]).astype(low)
-    release(slot_key)
-    put_t(5, low_tmp[...].T)
-    share_row(5)
-    low_tmp[...] = matmul(cols[10], banks[0].reshape(width, width)).astype(low)
-    low_tmp_two[...] = low_tmp[...].T
-    acc_t[...] = matmul(ring[slot_query], get_t(5)).reshape(blocks, PIECE, tokens)
-    release(slot_query)
-    reduce_step(1)
-
-    reduce_step(2)
+    state = {}
+
+    def value_back():
+        second[...] = matmul(ring[slot_value], get_t(0)).reshape(blocks, PIECE, tokens)
+        release(slot_value)
+
+        def mix_rows(p, carry):
+            zz, xx, cc = spot(p)
+            rows[1, zz, xx, cc] = second[p].astype(low)
+            return carry
+
+        over_pieces(mix_rows)
+        share_row(1)
+        acc_t[...] = matmul(banks[1].reshape(width, width), get_t(1)).reshape(blocks, PIECE, tokens)
+
+    def adapter_grads():
+        def share_rows(p, total):
+            return total + grouped(acc_t[p] * active[p]).sum(0)
+
+        share_grad = over_pieces(share_rows, jnp.zeros((adapters, tokens), jnp.float32))
+        logit_grad = shares * (share_grad - jnp.sum(shares * share_grad, 0, keepdims=True))
+        wide_logit = spread(logit_grad * score_scale)
+
+        def adapter_back(p, carry):
+            act_grad = acc_t[p] * wide_shares + wide_logit * acc_t_two[p]
+            where = pl.ds(p * PIECE, PIECE)
+            low_tmp_two[where, :] = (wide_logit * active[p]).astype(low)
+            bank_slope[p] = (bank_slope[p].astype(jnp.float32) * act_grad).astype(low)
+            return carry
+
+        over_pieces(adapter_back)
+        cols[9] = low_tmp_two[...].T
+        share_col(10)
+        cols[10] = bank_slope[...].reshape(width, tokens).T
+        share_col(11)
+
+    def probe_back():
+        cols[11] = matmul(cols[9], banks[1].reshape(width, width)).astype(low)
+        share_col(12)
+        low_tmp[...] = matmul(cols[11], ring[slot_key]).astype(low)
+        release(slot_key)
+        put_t(5, low_tmp[...].T)
+        share_row(5)
+        low_tmp[...] = matmul(cols[10], banks[0].reshape(width, width)).astype(low)
+        low_tmp_two[...] = low_tmp[...].T
+        acc_t[...] = matmul(ring[slot_query], get_t(5)).reshape(blocks, PIECE, tokens)
+        release(slot_query)
 
     def norm_back(index, gain, normed_ref, stat_ref, upstream_of, factor):
-        gain_col[...] = jnp.broadcast_to(gain[...], (128, width)).T.reshape(blocks, PIECE, 128)
+        gain_col[...] = jnp.broadcast_to(gain, (128, width)).T.reshape(blocks, PIECE, 128)
 
         def gained(p):
             column = gain_col[p]
@@ -712,16 +702,15 @@
 
     def upstream_two(p):
         zz, xx, cc = spot(p)
-        where = pl.ds(pl.multiple_of(p * PIECE, PIECE), PIECE)
+        where = pl.ds(p * PIECE, PIECE)
         total = rows[0, zz, xx, cc].astype(jnp.float32) + second[p]
         return total + low_tmp_two[where, :].astype(jnp.float32) + acc_t[p]
 
-    norm_back(1, gain_ff, norm_two, stat_two, upstream_two, 6)
-    share_row(6)
-    reduce_step(3)
-    reduce_step(4)
-
-    for k in range(4):
+    def norm_two_back():
+        norm_back(1, gain_ff, norm_two, stat_two, upstream_two, 6)
+        share_row(6)
+
+    def ff_back(k):
         slot = take()
         acc_t_two[...] = matmul(ring[slot], get_t(6)).reshape(blocks, PIECE, tokens)
         release(slot)
@@ -737,20 +726,19 @@
         value = value.reshape(blocks, PIECE, tokens)
         release(slot)
         acc_t[...] = value if k == 0 else acc_t[...] + value
-        reduce_step(5 + k)
-    for index in range(8, 12):
-        share_row(index)
+        if k == 3:
+            for index in range(8, 12):
+                share_row(index)
 
     def upstream_one(p):
         return second[p] + acc_t[p]
 
-    norm_back(0, gain_attn, norm_one, stat_one, upstream_one, 7)
-    share_row(7)
-    gain_copy = send(gain_sum.at[0], gain_from.at[0], gain_send.at[0], gain_recv.at[0], sibling)
-    slot = take()
-    low_tmp_two[...] = matmul(ring[slot], get_t(7)).astype(low)
-    release(slot)
-    reduce_step(9)
+    def norm_one_back():
+        norm_back(0, gain_attn, norm_one, stat_one, upstream_one, 7)
+        share_row(7)
+        slot = take()
+        low_tmp_two[...] = matmul(ring[slot], get_t(7)).astype(low)
+        release(slot)
 
     heads_step = 3
     step_pieces = heads_step * size // PIECE
@@ -776,60 +764,69 @@
                 rows_qkv[p // 12, (p // 6) % 2, (p % 6) // 2, p % 2] = stacked[i]
         return carry
 
-    lax.fori_loop(0, heads // heads_step, head_backward, 0)
-    for index in range(12, 15):
-        share_row(index)
-    for step in range(10, 14):
-        reduce_step(step)
-    gain_copy.wait_recv()
-    gain_sum[1] = gain_sum[0] + gain_from[0]
-    gain_copy = send(gain_sum.at[1], gain_from.at[1], gain_send.at[1], gain_recv.at[1], x_mate)
-    reduce_step(14)
-    reduce_step(15)
-    reduce_step(16)
-    for k in range(3):
-        slot = take()
-        block = rows_qkv[...].reshape(3 * blocks, PIECE, tokens)[k * blocks : (k + 1) * blocks]
-        value = matmul(ring[slot], block.reshape(width, tokens)).reshape(blocks, PIECE, tokens)
-        release(slot)
-        second[...] = second[...] + value
-    acc[...] = second[...].reshape(width, tokens).T
-    in_copy = pltpu.make_async_copy(acc, grad_in, local_sem.at[3])
-    in_copy.start()
-
-    for step in range(units, units + LAG_FOUR):
-        reduce_step(step)
-        if step == units:
-            gain_copy.wait_recv()
-            gain_sum[2] = gain_sum[1] + gain_from[1]
-            gain_copy = send(
-                gain_sum.at[2], gain_from.at[2], gain_send.at[2], gain_recv.at[2], y_mate
-            )
-        if step == units + 2:
-            gain_copy.wait_recv()
-            gain_sum[3] = gain_sum[2] + gain_from[2]
-            gain_copies = [
-                send(
-                    gain_sum.at[3],
-                    gain_from.at[3 + k],
-                    gain_send.at[3 + k],
-                    gain_recv.at[3 + k],
-                    z_mates[k],
-                )
-                for k in range(3)
-            ]
-        if step == units + 5:
-            total = gain_sum[3]
-            for k in range(3):
-                gain_copies[k].wait_recv()
-                total += gain_from[3 + k]
-            gain_sums[...] = total
+    def attention_back():
+        lax.fori_loop(0, heads // heads_step, head_backward, 0)
+        for index in range(12, 15):
+            share_row(index)
+
+    def input_back():
+        for k in range(3):
+            slot = take()
+            block = rows_qkv[...].reshape(3 * blocks, PIECE, tokens)[k * blocks : (k + 1) * blocks]
+            value = matmul(ring[slot], block.reshape(width, tokens)).reshape(blocks, PIECE, tokens)
+            release(slot)
+            second[...] = second[...] + value
+        acc[...] = second[...].reshape(width, tokens).T
+        state["in"] = pltpu.make_async_copy(acc, grad_in, local_sem.at[3])
+        state["in"].start()
+
+    gain_mates = (sibling, x_mate, y_mate, mates["l"], mates["h"])
+
+    def gain_step(stage):
+        if stage > 0:
+            state["gain"].wait_recv()
+            total = gain_sum[stage - 1] + gain_from[stage - 1]
+            if stage == 5:
+                gain_sums[...] = total
+                return
+            gain_sum[stage] = total
+        state["gain"] = send(
+            gain_sum.at[stage],
+            gain_from.at[stage],
+            gain_send.at[stage],
+            gain_recv.at[stage],
+            gain_mates[stage],
+        )
+
+    chain = [value_back, adapter_grads, probe_back, norm_two_back]
+    chain += [functools.partial(ff_back, k) for k in range(4)]
+    chain += [norm_one_back, attention_back, input_back]
+    progress = [0] * units
+    since_chain, gain_stage = 0, 0
+    for action in SEQUENCE:
+        if action < 0:
+            chain.pop(0)()
+        elif progress[action] == 0:
+            start(action)
+        elif progress[action] < 4:
+            advance(action, progress[action] - 1)
+        else:
+            close(action)
+        if action >= 0:
+            progress[action] += 1
+        if not chain:
+            if since_chain % 4 == 0 and gain_stage < 6:
+                gain_step(gain_stage)
+                gain_stage += 1
+            since_chain += 1
+    for stage in range(gain_stage, 6):
+        gain_step(stage)
     for unit in range(units):
         last[unit].wait_recv()
     for copy in started:
         copy.wait_send()
     out_copy.wait()
-    in_copy.wait()
+    state["in"].wait()
 
 
 def run_layer(heads, adapters, arrays):
@@ -884,23 +881,22 @@
             pltpu.VMEM((8, tokens), wide),
             pltpu.VMEM((8, tokens), wide),
             pltpu.VMEM((blocks, PIECE, 128), wide),
-            pltpu.VMEM((units, 2, 2, 4, PIECE, half_width), low),
-            pltpu.VMEM((units, 2, 4, PIECE, half_width), low),
-            pltpu.VMEM((units, 4, PIECE, half_width), low),
-            pltpu.VMEM((units, 3, PIECE, half_width), low),
-            pltpu.VMEM((4, 8, width), wide),
-            pltpu.VMEM((6, 8, width), wide),
+            pltpu.VMEM((units, 2, 2, 2, 2, PIECE, half_width), low),
+            pltpu.VMEM((units, 2, 2, 2, PIECE, half_width), low),
+            pltpu.VMEM((units, 2, 2, PIECE, half_width), low),
+            pltpu.VMEM((units, 2, PIECE, half_width), low),
+            pltpu.VMEM((units, PIECE, half_width), low),
+            pltpu.VMEM((5, 8, width), wide),
+            pltpu.VMEM((5, 8, width), wide),
             dma((SLOTS,)),
             dma((4,)),
         ]
         + pair((2, 3))
         + pair((15,))
         + pair((13,))
+        + pair((4, units))
         + pair((units,))
-        + pair((units,))
-        + pair((units, 3))
-        + pair((units,))
-        + pair((6,)),
+        + pair((5,)),
         compiler_params=pltpu.CompilerParams(
             collective_id=0, has_side_effects=True, vmem_limit_bytes=63 * 2**20
         ),
@@ -910,6 +906,10 @@
 def finish_kernel(
     sums,
     gain_sums,
+    output,
+    grad_in,
+    out_output,
+    out_grad_in,
     out_qkv,
     out_proj,
     out_gain_attn,
@@ -923,7 +923,14 @@
     out_up,
     out_gain_out,
     turned,
+    copy_sem,
 ):
+    passed = [
+        pltpu.make_async_copy(output, out_output, copy_sem.at[0]),
+        pltpu.make_async_copy(grad_in, out_grad_in, copy_sem.at[1]),
+    ]
+    for copy in passed:
+        copy.start()
     ad = lax.axis_index("ad")
     core = lax.axis_index("bn") % 2
     width = sums.shape[3]
@@ -945,52 +952,56 @@
     columns(out_qkv, 1, 14, 3)
     for i in range(2):
         value = sums[5 + 2 * core + i].reshape(2 * PIECE, width)
-        out_ff_out[pl.ds(i * width, width), :] = value.astype(jnp.float32).T
+        out_ff_out[:, pl.ds(i * width, width)] = value.astype(jnp.float32)
     total = gain_sums.shape[1]
-    piece = out_gain_attn.shape[1]
+    piece = out_gain_attn.shape[0]
     rolled = pltpu.roll(gain_sums[...], lax.rem(total - ad * piece, total), 1)[:, :piece]
-    out_gain_attn[...] = rolled[0:1]
-    out_gain_ff[...] = rolled[1:2]
-    out_gain_out[...] = rolled[2:3]
-
-
-def finish(sums, gain_sums, width):
+    for index, out in enumerate((out_gain_attn, out_gain_ff, out_gain_out)):
+        out[...] = rolled[index : index + 1].reshape(piece)
+    for copy in passed:
+        copy.wait()
+
+
+def finish(sums, gain_sums, output, grad_in, width):
     quarter, eighth = width // 4, width // 8
+    far = pl.BlockSpec(memory_space=pl.ANY)
     shapes = [
+        output.shape,
+        grad_in.shape,
         (quarter, 3 * eighth),
         (quarter, eighth),
-        (1, eighth),
+        (eighth,),
         (quarter, 4 * eighth),
-        (4 * quarter, eighth),
-        (1, eighth),
+        (eighth, 4 * quarter),
+        (eighth,),
     ]
-    shapes += [(quarter, eighth)] * 5 + [(1, eighth)]
+    shapes += [(quarter, eighth)] * 5 + [(eighth,)]
     return pl.pallas_call(
         finish_kernel,
         out_shape=tuple(jax.ShapeDtypeStruct(shape, jnp.float32) for shape in shapes),
-        in_specs=[pl.BlockSpec(memory_space=pltpu.VMEM)] * 2,
-        out_specs=[pl.BlockSpec(memory_space=pltpu.VMEM)] * 12,
-        scratch_shapes=[pltpu.VMEM((3, width // 2, 4 * eighth), jnp.float32)],
+        in_specs=[pl.BlockSpec(memory_space=pltpu.VMEM)] * 2 + [far] * 2,
+        out_specs=[far] * 2 + [pl.BlockSpec(memory_space=pltpu.VMEM)] * 12,
+        scratch_shapes=[
+            pltpu.VMEM((3, width // 2, 4 * eighth), jnp.float32),
+            pltpu.SemaphoreType.DMA((2,)),
+        ],
         compiler_params=pltpu.CompilerParams(vmem_limit_bytes=32 * 2**20),
-    )(sums, gain_sums)
+    )(sums, gain_sums, output, grad_in)
 
 
 def fast_local(*arrays):
     arrays = list(arrays)
     width = arrays[0].shape[1]
     adapters = arrays[12].shape[1]
-    for i in (5, 8, 14):
-        arrays[i] = arrays[i].reshape(1, width)
     bank_shape = arrays[12].shape[:2] + (-1,)
     for i in (12, 13):
         arrays[i] = arrays[i].reshape(-1, width)
     output, grad_in, sums, gain_sums = run_layer(H, adapters, arrays)
-    grads = list(finish(sums, gain_sums, width))
-    for i in (2, 5, 11):
-        grads[i] = grads[i].reshape(-1)
-    for i in (9, 10):
-        grads[i] = grads[i].reshape(bank_shape)
-    return (output, grad_in, *grads)
+    results = list(finish(sums, gain_sums, output, grad_in, width))
+    results[6] = results[6].T
+    for i in (11, 12):
+        results[i] = results[i].reshape(bank_shape)
+    return tuple(results)
 
 
 def local(

time: 149 us -> 128 us (0.86)
  Pallas kernels: 139 us -> 122 us
  local copies, waits for them, and re-layouts: 8.47 us -> 4.29 us
    pallas_call x1, Pallas kernels: 137 us -> 120 us  [run_layer(): pl.pallas_call(functools.partial(layer_kernel, heads, adapters), out_shap...]
    reshape x3 -> x0, local copies, waits for them, and re-layouts: 3.8 us -> none  [fast_local(): arrays[i] = arrays[i].reshape(1, width)]
    unnamed x11 -> x8, local copies, waits for them, and re-layouts: 4.67 us -> 4.29 us
where the time goes in v1:
time: 128 us
  Pallas kernels  122 us (95%)
  local copies, waits for them, and re-layouts  4.29 us (3%)
  between operations  1.5 us (1%)
    pallas_call x1, Pallas kernels, run_layer(): pl.pallas_call(functools.partial(layer_kernel, heads, adapters), out_shap...  120 us
    unnamed x8, local copies, waits for them, and re-layouts  4.29 us

profile of v1, /device:TPU:0, one launch (start us, length us, event | category | flops | bytes accessed | tf_op | source)
XLA Modules:
  0.0 127.8 jit_solution(8768757807734685569)
XLA Ops:
  1.3 119.7 %shard_map.254 = (f32[256,768]{1,0:T(8,128)}, f32[256,768]{1,0:T(8,128)}, bf16[17,2,48,384]{3,2,1,0:T(8,128)(2,1)}, f32[8,768]{1,0:T(8,128)}) custom-call(bf16[256,768]{1,0:T(8,128)(2,1)} %hidden.1, s32[1]{0:T(128)S(6)} %copy.29.lengths, bf16[256,768]{1,0:T(8,128)(2,1)} %cotangent.1, bf16[768,2304]{1,0:T(8,128)(2,1)} %w_qkv.1, bf16[768,768]{1,0:T(8,128)(2,1)} %w_out.1, ...), custom_call_target="tpu_custom_call" | custom-call | tf_op jit(solution)/shard_map/pallas_call | solution.py:844
  121.0 0.0 copy-start
  121.0 1.3 %copy-done = bf16[17,2,48,384]{3,2,1,0:T(8,128)(2,1)S(1)} copy-done((bf16[17,2,48,384]{3,2,1,0:T(8,128)(2,1)S(1)}, bf16[17,2,48,384]{3,2,1,0:T(8,128)(2,1)}, u32[]{:S(2)}) %copy-start) | copy-done | bytes 1253400
  122.3 0.0 copy-start.1
  122.3 1.1 copy-done.1
  123.5 0.0 copy-start.2
  123.5 1.1 copy-done.2
  124.6 0.0 copy-start.3
  124.6 0.7 copy-done.3
  125.3 2.3 %shard_map.255 = (f32[256,768]{1,0:T(8,128)}, f32[256,768]{1,0:T(8,128)}, f32[192,288]{1,0:T(8,128)}, f32[192,96]{1,0:T(8,128)}, f32[96]{0:T(128)}, /*index=5*/f...) custom-call(bf16[17,2,48,384]{3,2,1,0:T(8,128)(2,1)S(1)} %copy-done,, ...), custom_call_target="tpu_custom_call" | custom-call | tf_op jit(solution)/shard_map/pallas_call | solution.py:979
Async XLA Ops:
  121.0 1.3 %copy-start = (bf16[17,2,48,384]{3,2,1,0:T(8,128)(2,1)S(1)}, bf16[17,2,48,384]{3,2,1,0:T(8,128)(2,1)}, u32[]{:S(2)}) copy-start(bf16[17,2,48,384]{3,2,1,0:T(8,128)(2,1)} %get-tuple-element.32.sums) | copy-start | bytes 3760132
  122.3 1.1 copy-start.1
  123.5 1.1 copy-start.2
  124.6 0.7 copy-start.3

commit v2 on v1

--- a/solution.py
+++ b/solution.py
@@ -81,6 +81,7 @@
 
 PIECE = 48
 SLOTS = 5
+SENDS = 48
 UNITS = (
     ((0, 8),),
     ((1, 9), (2, 10)),
@@ -102,30 +103,33 @@
 )
 
 
+CROSS_X = (9, 10, 11, 12, 14, 15, 16)
+CROSS_Y = (5, 6, 7, 8)
+WHOLE = tuple(unit for unit in range(len(UNITS)) if unit not in CROSS_X + CROSS_Y)
 ORDERS = (
+    ("x", "y", "l", "h"),
+    ("l", "y", "x", "h"),
+    ("l", "h", "x", "y"),
+    ("y", "l", "x", "h"),
+    ("x", "y", "l", "h"),
+    ("y", "l", "h", "x"),
     ("y", "x", "l", "h"),
-    ("l", "y", "x", "h"),
+    ("y", "l", "h", "x"),
+    ("y", "l", "x", "h"),
     ("x", "l", "h", "y"),
-    ("y", "x", "l", "h"),
-    ("y", "l", "x", "h"),
-    ("y", "l", "x", "h"),
-    ("l", "x", "y", "h"),
-    ("x", "l", "h", "y"),
-    ("y", "x", "l", "h"),
-    ("x", "l", "h", "y"),
-    ("x", "l", "y", "h"),
-    ("l", "x", "h", "y"),
+    ("x", "y", "l", "h"),
+    ("x", "y", "l", "h"),
+    ("x", "y", "l", "h"),
     ("y", "x", "l", "h"),
     ("x", "y", "l", "h"),
-    ("y", "x", "l", "h"),
-    ("y", "l", "x", "h"),
+    ("x", "y", "l", "h"),
     ("x", "y", "l", "h"),
 )
 SEQUENCE = (
-    -1, -1, 0, -1, 2, 1, -1, 3, -1, 7, 6, 8, -1, -1, -1, 0, -1, 2, 9, 11, 4, -1, 13, 5,
-    -1, 2, 16, 0, 15, 7, 9, 10, 14, 0, 4, 7, 5, 12, 0, 3, 9, 15, 4, 11, 10, 5, 2, 7, 3,
-    8, 9, 16, 4, 15, 13, 11, 14, 2, 5, 3, 7, 4, 9, 10, 6, 1, 8, 16, 5, 15, 12, 11, 3, 8,
-    13, 16, 14, 15, 10, 8, 13, 6, 16, 1, 11, 14, 10, 12, 6, 13, 1, 14, 12, 6, 1, 12,
+    -1, -1, 0, -1, 2, -1, 1, 3, 4, -1, -1, 8, 6, 7, 5, -1, -1, -1, 2, 9, 10, -1, 4, 3,
+    12, -1, 0, 14, 9, 13, 8, 7, 16, 5, 10, 15, 4, 9, 12, 0, 11, 7, 14, 5, 16, 8, 4, 10,
+    2, 9, 3, 0, 15, 12, 6, 1, 4, 14, 7, 5, 10, 8, 13, 0, 11, 16, 12, 9, 3, 14, 2, 10,
+    15, 8, 6, 16, 7, 12, 5, 1, 3, 14, 15, 13, 11, 6, 2, 1, 16, 15, 13, 11, 6, 1, 13, 11,
 )
 
 def flip(index, bit):
@@ -143,7 +147,7 @@
     adapters,
     hidden,
     lengths,
-    cotangent,
+    cotangent_far,
     w_qkv,
     w_out,
     gain_attn,
@@ -166,6 +170,10 @@
     rows_sib,
     cols,
     cols_sib,
+    rows_x,
+    cols_x,
+    rows_y,
+    cols_y,
     ring,
     banks,
     acc,
@@ -187,6 +195,7 @@
     stat_one,
     stat_two,
     gain_col,
+    cotangent,
     part,
     recv_one,
     recv_two,
@@ -196,17 +205,16 @@
     gain_from,
     ring_sem,
     local_sem,
-    bank_send,
+    send_sem,
     bank_recv,
-    row_send,
     row_recv,
-    col_send,
     col_recv,
-    stage_send,
+    row_x_recv,
+    col_x_recv,
+    row_y_recv,
+    col_y_recv,
     stage_recv,
-    last_send,
     last_recv,
-    gain_send,
     gain_recv,
 ):
     low = jnp.bfloat16
@@ -258,10 +266,19 @@
         fill()
 
     fill()
+    upstream_copy = pltpu.make_async_copy(cotangent_far, cotangent, local_sem.at[6])
+    upstream_copy.start()
     bank_own = []
     for i, bank in enumerate((adapt_down, adapt_up)):
-        bank_own.append(pltpu.make_async_copy(bank, banks.at[i, bn], local_sem.at[i]))
-        bank_own[i].start()
+        for side in range(2):
+            bank_own.append(
+                pltpu.make_async_copy(
+                    bank.at[pl.ds(side * (width // 8), width // 8), :],
+                    banks.at[i, bn, side],
+                    local_sem.at[2 + 2 * i + side],
+                )
+            )
+            bank_own[-1].start()
 
     barrier = pltpu.get_barrier_semaphore()
     for mate in [sibling, *mates.values()]:
@@ -269,11 +286,14 @@
 
     started = []
 
-    def send(source, target, send_sem, recv_sem, mate):
+    def send(source, target, recv_sem, mate):
+        slot = len(started) % SENDS
+        if len(started) >= SENDS:
+            started[-SENDS].wait_send()
         copy = pltpu.make_async_remote_copy(
             src_ref=source,
             dst_ref=target,
-            send_sem=send_sem,
+            send_sem=send_sem.at[slot],
             recv_sem=recv_sem,
             device_id=mate,
             device_id_type=MESH,
@@ -308,7 +328,6 @@
         row_copies[index] = send(
             row_views(index).at[:, :, other_core],
             rows_sib.at[index],
-            row_send.at[index],
             row_recv.at[index],
             sibling,
         )
@@ -317,10 +336,95 @@
         col_copies[index] = send(
             col_ref(index),
             cols_sib.at[index],
-            col_send.at[index],
             col_recv.at[index],
             sibling,
         )
+
+    cross = {}
+    lanes_of = [
+        pl.ds(pl.multiple_of(side * half_width, half_width), half_width) for side in (y, 1 - y)
+    ]
+
+    def cross_send(key, source, target, sem, index, mate):
+        cross[key] = send(source, target, sem.at[index], mate)
+
+    def col_over_x(i):
+        cross_send(("cx", i), col_ref(2 * i), cols_x.at[0, i], col_x_recv, (0, i), x_mate)
+
+    def col_over_y(k):
+        source = cols.at[2 + k, :, lanes_of[1]]
+        cross_send(("cy", k), source, cols_y.at[0, k], col_y_recv, (0, k), y_mate)
+
+    def need(copy_key, table=cross):
+        if (id(table), copy_key) not in arrived:
+            table[copy_key].wait_recv()
+            arrived.add((id(table), copy_key))
+
+    def pass_col_x(i):
+        if ("fx", i) not in cross:
+            need(("cx", i))
+            cross_send(
+                ("fx", i), cols_x.at[0, i], cols_x.at[1, i], col_x_recv, (1, i), sibling
+            )
+
+    def pass_col_y(k):
+        need(("cy", k))
+        cross_send(
+            ("fy", k), cols_y.at[0, k], cols_y.at[1, k], col_y_recv, (1, k), sibling
+        )
+
+    def start_x(unit):
+        left, right = UNITS[unit][0]
+        n = left - 8
+        sem = row_x_recv
+        source = row_views(left).at[:, 1 - x, core]
+        cross_send(("rx", n, 0), source, rows_x.at[0, n], sem, (0, n), x_mate)
+        pass_col_x(right // 2)
+        need(left, row_copies)
+        cross_send(
+            ("rx", n, 1), rows_sib.at[left, :, 1 - x], rows_x.at[1, n], sem, (1, n), x_mate
+        )
+
+    def product_x(unit):
+        left, right = UNITS[unit][0]
+        n, i = left - 8, right // 2
+        need(right, col_copies)
+        need(("fx", i))
+        flat = (4 * PIECE, tokens)
+        total = matmul(row_half(left, x), col_ref(right)[...])
+        total += matmul(rows_sib[left, :, x].reshape(flat), cols_sib[right])
+        for k in range(2):
+            need(("rx", n, k))
+            total += matmul(rows_x[k, n].reshape(flat), cols_x[k, i])
+        total = total.astype(low).reshape(2, 2, PIECE, width)
+        part[unit, 0, x] = total[..., :half_width]
+        part[unit, 1, x] = total[..., half_width:]
+
+    def start_y(unit):
+        if ("ry", 0) not in cross:
+            sem = row_y_recv
+            cross_send(("ry", 0), rows.at[6, :, :, core], rows_y.at[0], sem, 0, y_mate)
+            for k in range(4):
+                pass_col_y(k)
+            need(6, row_copies)
+            cross_send(("ry", 1), rows_sib.at[6], rows_y.at[1], sem, 1, y_mate)
+
+    def product_y(unit):
+        left, right = UNITS[unit][0]
+        k = right - 3
+        need(right, col_copies)
+        need(("fy", k))
+        flat = (4 * PIECE, tokens)
+        for i in range(2):
+            need(("ry", i))
+        for side in range(2):
+            total = matmul(row_half(left, side), cols[2 + k, :, lanes_of[0]])
+            total += matmul(
+                rows_sib[left, :, side].reshape(flat), cols_sib[right, :, lanes_of[0]]
+            )
+            for i in range(2):
+                total += matmul(rows_y[i, :, side].reshape(flat), cols_y[i, k])
+            part[unit, y, side] = total.astype(low).reshape(2, 2, PIECE, half_width)
 
     axes = ("y", "x", "h", "l")
     recvs = (recv_one, recv_two, recv_three, recv_four)
@@ -330,12 +434,8 @@
     def half(unit, side):
         total = None
         for left, right in UNITS[unit]:
-            if (0, left) not in arrived:
-                row_copies[left].wait_recv()
-                arrived.add((0, left))
-            if (1, right) not in arrived:
-                col_copies[right].wait_recv()
-                arrived.add((1, right))
+            need(left, row_copies)
+            need(right, col_copies)
             term = matmul(row_half(left, side), col_ref(right)[...])
             term += matmul(
                 rows_sib[left, :, side].reshape(4 * PIECE, tokens), cols_sib[right]
@@ -352,20 +452,26 @@
         inside = tuple(index if name == axis else slice(None) for name in left)
         return tuple(fixed.get(name, slice(None)) for name in axes), inside
 
+    def landing(unit, stage):
+        return WHOLE.index(unit) if stage == 0 else unit
+
     def push(unit, stage):
         order = ORDERS[unit]
         axis = order[stage]
         where, _ = place(order[:stage], axis, 1 - own[axis])
         copies[unit, stage] = send(
             part.at[(unit, *where)],
-            recvs[stage].at[unit],
-            stage_send.at[stage, unit],
+            recvs[stage].at[landing(unit, stage)],
             stage_recv.at[stage, unit],
             mates[axis],
         )
 
     def start(unit):
-        if ORDERS[unit][0] == "x":
+        if unit in CROSS_X:
+            start_x(unit)
+        elif unit in CROSS_Y:
+            start_y(unit)
+        elif ORDERS[unit][0] == "x":
             half(unit, 1 - x)
             push(unit, 0)
             half(unit, x)
@@ -377,9 +483,16 @@
     def add(unit, stage, axis, index):
         where, inside = place(ORDERS[unit][: stage + 1], axis, index)
         mine = part[(unit, *where)].astype(jnp.float32)
-        part[(unit, *where)] = (mine + recvs[stage][(unit, *inside)].astype(jnp.float32)).astype(low)
+        part[(unit, *where)] = (mine + recvs[stage][(landing(unit, stage), *inside)].astype(jnp.float32)).astype(low)
 
     def advance(unit, stage):
+        if stage == 0 and unit not in WHOLE:
+            if unit in CROSS_X:
+                product_x(unit)
+            else:
+                product_y(unit)
+            push(unit, 1)
+            return
         copies[unit, stage].wait_recv()
         axis = ORDERS[unit][stage + 1]
         add(unit, stage, axis, 1 - own[axis])
@@ -393,7 +506,6 @@
         last[unit] = send(
             sums.at[unit, core],
             sums.at[unit, core],
-            last_send.at[unit],
             last_recv.at[unit],
             sibling,
         )
@@ -429,15 +541,38 @@
             value = value * 0.125
         qkv_t[pl.ds(k * width, width), :] = value.astype(low).T
     pl.semaphore_wait(barrier, 1 + len(mates))
-    bank_sib, bank_y, bank_far = [], [], []
-    for i, bank in enumerate((adapt_down, adapt_up)):
-        bank_y.append(
-            send(bank, banks.at[i, bn], bank_send.at[i, 1], bank_recv.at[i, 1], y_mate)
+    banks_in = (adapt_down, adapt_up)
+    half_bank = width // 8
+    far = flip(bn, 2)
+
+    def bank_half(bank, side):
+        return bank.at[pl.ds(pl.multiple_of(side * half_bank, half_bank), half_bank), :]
+
+    bank_y, bank_x, bank_sib = [], [], []
+
+    def send_bank(source, i, where, kind, mate):
+        return send(
+            source, banks.at[(i, *where)], bank_recv.at[i, kind], mate
         )
-    for i, bank in enumerate((adapt_down, adapt_up)):
-        bank_sib.append(
-            send(bank, banks.at[i, bn], bank_send.at[i, 0], bank_recv.at[i, 0], sibling)
-        )
+
+    for i in range(2):
+        bank_y.append(send_bank(bank_half(banks_in[i], x), i, (bn, x), 0, y_mate))
+    for i in range(2):
+        for side in range(2):
+            source = bank_half(banks_in[i], side)
+            bank_sib.append(send_bank(source, i, (bn, side), 1 + side, sibling))
+
+    def pass_from_y(i):
+        bank_y[i].wait_recv()
+        source = banks.at[i, far, x]
+        bank_x.append(send_bank(source, i, (far, x), 3, x_mate))
+        bank_sib.append(send_bank(source, i, (far, x), 4, sibling))
+
+    def pass_from_x(i):
+        bank_x[i].wait_recv()
+        source = banks.at[i, far, 1 - x]
+        bank_sib.append(send_bank(source, i, (far, 1 - x), 5, sibling))
+
     share_col(0)
     size = width // heads
 
@@ -457,6 +592,7 @@
         return carry
 
     lax.fori_loop(0, heads, head_forward, 0, unroll=3)
+    pass_from_y(0)
     cols[0] = low_tmp_two[...].T
     share_col(1)
     slot = take()
@@ -505,19 +641,14 @@
         value = matmul(low_tmp[...], ring[slot])
         release(slot)
         acc_two[...] = value if k == 0 else acc_two[...] + value
-        if k == 1:
+        if k == 0:
+            pass_from_y(1)
             for i in range(2):
-                bank_y[i].wait_recv()
-                far = flip(bn, 2)
-                bank_far.append(
-                    send(
-                        banks.at[i, far],
-                        banks.at[i, far],
-                        bank_send.at[i, 2],
-                        bank_recv.at[i, 2],
-                        sibling,
-                    )
-                )
+                col_over_x(i)
+        if k == 2:
+            pass_from_x(0)
+    for k in range(4):
+        col_over_y(k)
     for index in range(3, 7):
         share_col(index)
 
@@ -537,6 +668,7 @@
     put_t(3, cols[6].T)
     share_row(3)
 
+    pass_from_x(1)
     slot_query = take()
     low_tmp[...] = matmul(cols[6], ring[slot_query]).astype(low)
     put_t(4, low_tmp[...].T)
@@ -545,10 +677,10 @@
     put_t(2, matmul(ring[slot_key], get_t(4)).astype(low))
     share_row(2)
 
-    for i in range(2):
-        bank_own[i].wait()
-        bank_sib[i].wait_recv()
-        bank_far[i].wait_recv()
+    for copy in bank_own:
+        copy.wait()
+    for copy in bank_sib:
+        copy.wait_recv()
     acc_t[...] = matmul(banks[0].reshape(width, width), get_t(3)).reshape(blocks, PIECE, tokens)
     acc_t_two[...] = matmul(banks[1].reshape(width, width), get_t(2)).reshape(
         blocks, PIECE, tokens
@@ -595,6 +727,8 @@
     share_col(8)
     slot_value = take()
     acc[...] = matmul(cols[7], ring[slot_value])
+
+    upstream_copy.wait()
 
     def norm_third(r, i, gain_part):
         normed, rstd = norm_rows(wide[r, :] + acc[r, :])
@@ -613,7 +747,7 @@
         return gain_part + product.reshape(step_rows // 8, 8, width).sum(0)
 
     gain_part = over_rows(norm_third, jnp.zeros((8, width), jnp.float32))
-    out_copy = pltpu.make_async_copy(acc_two, output, local_sem.at[2])
+    out_copy = pltpu.make_async_copy(acc_two, output, local_sem.at[0])
     out_copy.start()
     gain_sum[0] = jnp.broadcast_to(jnp.sum(gain_part, 0, keepdims=True), (8, width))
     put_t(0, low_tmp[...].T)
@@ -777,7 +911,7 @@
             release(slot)
             second[...] = second[...] + value
         acc[...] = second[...].reshape(width, tokens).T
-        state["in"] = pltpu.make_async_copy(acc, grad_in, local_sem.at[3])
+        state["in"] = pltpu.make_async_copy(acc, grad_in, local_sem.at[1])
         state["in"].start()
 
     gain_mates = (sibling, x_mate, y_mate, mates["l"], mates["h"])
@@ -793,7 +927,6 @@
         state["gain"] = send(
             gain_sum.at[stage],
             gain_from.at[stage],
-            gain_send.at[stage],
             gain_recv.at[stage],
             gain_mates[stage],
         )
@@ -823,7 +956,7 @@
         gain_step(stage)
     for unit in range(units):
         last[unit].wait_recv()
-    for copy in started:
+    for copy in started[-SENDS:]:
         copy.wait_send()
     out_copy.wait()
     state["in"].wait()
@@ -840,7 +973,6 @@
     smem = pl.BlockSpec(memory_space=pltpu.SMEM)
     far = pl.BlockSpec(memory_space=pl.ANY)
     half_width = width // 2
-    pair = lambda shape: [dma(shape), dma(shape)]
     return pl.pallas_call(
         functools.partial(layer_kernel, heads, adapters),
         out_shape=(
@@ -850,7 +982,7 @@
             jax.ShapeDtypeStruct((8, width), wide),
         ),
         in_specs=[
-            vmem, smem, vmem, far, far, vmem, far, far, vmem, far, far, far, far, far, vmem,
+            vmem, smem, far, far, far, vmem, far, far, vmem, far, far, far, far, far, vmem,
         ],
         out_specs=[far, far, vmem, vmem],
         scratch_shapes=[
@@ -860,8 +992,12 @@
             pltpu.VMEM((15, 4, 2, PIECE, tokens), low),
             pltpu.VMEM((12, tokens, width), low),
             pltpu.VMEM((13, tokens, width), low),
+            pltpu.VMEM((2, 7, 4, PIECE, tokens), low),
+            pltpu.VMEM((2, 2, tokens, width), low),
+            pltpu.VMEM((2, 4, 2, PIECE, tokens), low),
+            pltpu.VMEM((2, 4, tokens, half_width), low),
             pltpu.VMEM((SLOTS, width, width), low),
-            pltpu.VMEM((2, 4, width // 4, width), low),
+            pltpu.VMEM((2, 4, 2, width // 8, width), low),
             pltpu.VMEM((tokens, width), wide),
             pltpu.VMEM((tokens, width), wide),
             pltpu.VMEM((tokens, width), wide),
@@ -881,22 +1017,28 @@
             pltpu.VMEM((8, tokens), wide),
             pltpu.VMEM((8, tokens), wide),
             pltpu.VMEM((blocks, PIECE, 128), wide),
+            pltpu.VMEM((tokens, width), low),
             pltpu.VMEM((units, 2, 2, 2, 2, PIECE, half_width), low),
-            pltpu.VMEM((units, 2, 2, 2, PIECE, half_width), low),
+            pltpu.VMEM((len(WHOLE), 2, 2, 2, PIECE, half_width), low),
             pltpu.VMEM((units, 2, 2, PIECE, half_width), low),
             pltpu.VMEM((units, 2, PIECE, half_width), low),
             pltpu.VMEM((units, PIECE, half_width), low),
             pltpu.VMEM((5, 8, width), wide),
             pltpu.VMEM((5, 8, width), wide),
             dma((SLOTS,)),
-            dma((4,)),
-        ]
-        + pair((2, 3))
-        + pair((15,))
-        + pair((13,))
-        + pair((4, units))
-        + pair((units,))
-        + pair((5,)),
+            dma((7,)),
+            dma((SENDS,)),
+            dma((2, 6)),
+            dma((15,)),
+            dma((13,)),
+            dma((2, 7)),
+            dma((2, 2)),
+            dma((2,)),
+            dma((2, 4)),
+            dma((4, units)),
+            dma((units,)),
+            dma((5,)),
+        ],
         compiler_params=pltpu.CompilerParams(
             collective_id=0, has_side_effects=True, vmem_limit_bytes=63 * 2**20
         ),
@@ -904,8 +1046,8 @@
 
 
 def finish_kernel(
-    sums,
-    gain_sums,
+    sums_far,
+    gain_sums_far,
     output,
     grad_in,
     out_output,
@@ -923,14 +1065,23 @@
     out_up,
     out_gain_out,
     turned,
+    sums,
+    gain_sums,
+    held,
     copy_sem,
 ):
-    passed = [
-        pltpu.make_async_copy(output, out_output, copy_sem.at[0]),
-        pltpu.make_async_copy(grad_in, out_grad_in, copy_sem.at[1]),
+    fetched = [
+        pltpu.make_async_copy(sums_far, sums, copy_sem.at[2]),
+        pltpu.make_async_copy(gain_sums_far, gain_sums, copy_sem.at[3]),
     ]
-    for copy in passed:
+    through = [
+        pltpu.make_async_copy(output, held.at[0], copy_sem.at[0]),
+        pltpu.make_async_copy(grad_in, held.at[1], copy_sem.at[1]),
+    ]
+    for copy in fetched + through:
         copy.start()
+    for copy in fetched:
+        copy.wait()
     ad = lax.axis_index("ad")
     core = lax.axis_index("bn") % 2
     width = sums.shape[3]
@@ -947,6 +1098,14 @@
     columns(out_down, 2, 2, 1)
     columns(out_key, 0, 3, 1)
     columns(out_query, 1, 4, 1)
+    for copy in through:
+        copy.wait()
+    passed = [
+        pltpu.make_async_copy(held.at[0], out_output, copy_sem.at[0]),
+        pltpu.make_async_copy(held.at[1], out_grad_in, copy_sem.at[1]),
+    ]
+    for copy in passed:
+        copy.start()
     columns(out_ff_in, 2, 9, 4)
     columns(out_proj, 0, 13, 1)
     columns(out_qkv, 1, 14, 3)
@@ -979,13 +1138,16 @@
     return pl.pallas_call(
         finish_kernel,
         out_shape=tuple(jax.ShapeDtypeStruct(shape, jnp.float32) for shape in shapes),
-        in_specs=[pl.BlockSpec(memory_space=pltpu.VMEM)] * 2 + [far] * 2,
+        in_specs=[far] * 4,
         out_specs=[far] * 2 + [pl.BlockSpec(memory_space=pltpu.VMEM)] * 12,
         scratch_shapes=[
             pltpu.VMEM((3, width // 2, 4 * eighth), jnp.float32),
-            pltpu.SemaphoreType.DMA((2,)),
+            pltpu.VMEM(sums.shape, sums.dtype),
+            pltpu.VMEM(gain_sums.shape, gain_sums.dtype),
+            pltpu.VMEM((2, *output.shape), output.dtype),
+            pltpu.SemaphoreType.DMA((4,)),
         ],
-        compiler_params=pltpu.CompilerParams(vmem_limit_bytes=32 * 2**20),
+        compiler_params=pltpu.CompilerParams(vmem_limit_bytes=62 * 2**20),
     )(sums, gain_sums, output, grad_in)
 
 

time: 128 us -> 116 us (0.906)
  Pallas kernels: 122 us -> 113 us
  local copies, waits for them, and re-layouts: 4.29 us -> 0 us
    pallas_call x1, Pallas kernels: 120 us -> 109 us  [run_layer(): pl.pallas_call(functools.partial(layer_kernel, heads, adapters), out_shap...]
    unnamed x8 -> x0, local copies, waits for them, and re-layouts: 4.29 us -> none
    pallas_call x1, Pallas kernels: 2.29 us -> 4.05 us  [finish(): pl.pallas_call(finish_kernel, out_shape=tuple((jax.ShapeDtypeStruct(shape...]
where the time goes in v2:
time: 116 us; the launch traced here: 115 us
  Pallas kernels  113 us (97%)
  between operations  1.48 us (1%)
    pallas_call x1, Pallas kernels, run_layer(): pl.pallas_call(functools.partial(layer_kernel, heads, adapters), out_shap...  109 us
    pallas_call x1, Pallas kernels, finish(): pl.pallas_call(finish_kernel, out_shape=tuple((jax.ShapeDtypeStruct(shape...  4.05 us

profile of v2, /device:TPU:0, one launch (start us, length us, event | category | flops | bytes accessed | tf_op | source)
XLA Modules:
  0.0 114.9 jit_solution(1894268241749134161)
XLA Ops:
  1.3 109.4 %shard_map.254 = (f32[256,768]{1,0:T(8,128)}, f32[256,768]{1,0:T(8,128)}, bf16[17,2,48,384]{3,2,1,0:T(8,128)(2,1)}, f32[8,768]{1,0:T(8,128)}) custom-call(bf16[256,768]{1,0:T(8,128)(2,1)} %hidden.1, s32[1]{0:T(128)S(6)} %copy.29.lengths, bf16[256,768]{1,0:T(8,128)(2,1)} %cotangent_far.1, bf16[768,2304]{1,0:T(8,128)(2,1)} %w_qkv.1, bf16[768,768]{1,0:T(8,128)(2,1)} %w_out.1, ...), custom_call_target="tpu_custom_call" | custom-call | tf_op jit(solution)/shard_map/pallas_call | solution.py:976
  110.7 4.0 %shard_map.255 = (f32[256,768]{1,0:T(8,128)}, f32[256,768]{1,0:T(8,128)}, f32[192,288]{1,0:T(8,128)}, f32[192,96]{1,0:T(8,128)}, f32[96]{0:T(128)}, /*index=5*/f...) custom-call(bf16[17,2,48,384]{3,2,1,0:T(8,128)(2,1)} %get-tuple-elem, ...), custom_call_target="tpu_custom_call" | custom-call | tf_op jit(solution)/shard_map/pallas_call | solution.py:1138

commit v3 on v2

--- a/solution.py
+++ b/solution.py
@@ -107,29 +107,29 @@
 CROSS_Y = (5, 6, 7, 8)
 WHOLE = tuple(unit for unit in range(len(UNITS)) if unit not in CROSS_X + CROSS_Y)
 ORDERS = (
+    ("l", "y", "x", "h"),
+    ("y", "l", "x", "h"),
+    ("l", "y", "x", "h"),
+    ("x", "l", "y", "h"),
+    ("l", "x", "y", "h"),
+    ("y", "l", "x", "h"),
+    ("y", "l", "x", "h"),
+    ("y", "x", "l", "h"),
+    ("y", "x", "l", "h"),
     ("x", "y", "l", "h"),
-    ("l", "y", "x", "h"),
-    ("l", "h", "x", "y"),
-    ("y", "l", "x", "h"),
-    ("x", "y", "l", "h"),
-    ("y", "l", "h", "x"),
-    ("y", "x", "l", "h"),
-    ("y", "l", "h", "x"),
-    ("y", "l", "x", "h"),
-    ("x", "l", "h", "y"),
+    ("x", "l", "y", "h"),
     ("x", "y", "l", "h"),
     ("x", "y", "l", "h"),
-    ("x", "y", "l", "h"),
-    ("y", "x", "l", "h"),
+    ("y", "l", "x", "h"),
     ("x", "y", "l", "h"),
     ("x", "y", "l", "h"),
     ("x", "y", "l", "h"),
 )
 SEQUENCE = (
-    -1, -1, 0, -1, 2, -1, 1, 3, 4, -1, -1, 8, 6, 7, 5, -1, -1, -1, 2, 9, 10, -1, 4, 3,
-    12, -1, 0, 14, 9, 13, 8, 7, 16, 5, 10, 15, 4, 9, 12, 0, 11, 7, 14, 5, 16, 8, 4, 10,
-    2, 9, 3, 0, 15, 12, 6, 1, 4, 14, 7, 5, 10, 8, 13, 0, 11, 16, 12, 9, 3, 14, 2, 10,
-    15, 8, 6, 16, 7, 12, 5, 1, 3, 14, 15, 13, 11, 6, 2, 1, 16, 15, 13, 11, 6, 1, 13, 11,
+    -1, -1, -1, 0, 1, -1, 3, 2, -1, 6, 7, 5, 8, -1, -1, -1, 4, -1, 9, 12, -1, 0, 11, -1,
+    1, 9, 16, 3, 13, 6, 14, 5, 10, 12, 9, 3, 15, 16, 13, 11, 1, 12, 9, 6, 14, 3, 10, 0,
+    13, 2, 16, 12, 5, 9, 3, 7, 15, 1, 11, 6, 4, 10, 0, 14, 16, 12, 13, 1, 8, 5, 11, 6,
+    0, 2, 7, 15, 14, 16, 10, 13, 5, 4, 11, 7, 8, 15, 4, 14, 2, 10, 7, 8, 15, 4, 2, 8,
 )
 
 def flip(index, bit):
@@ -211,6 +211,7 @@
     col_recv,
     row_x_recv,
     col_x_recv,
+    hidden_x_recv,
     row_y_recv,
     col_y_recv,
     stage_recv,
@@ -236,9 +237,11 @@
     other_core = 1 - core
 
     loads = [(w_qkv.at[:, pl.ds(k * width, width)]) for k in range(3)] + [w_out]
-    for k in range(4):
-        loads.append(w_ff_in.at[:, pl.ds(k * width, width)])
-        loads.append(w_ff_out.at[pl.ds(k * width, width), :])
+    ff_blocks = [2 * (1 - y), 2 * (1 - y) + 1, 2 * y, 2 * y + 1]
+    for block in ff_blocks:
+        where = pl.ds(pl.multiple_of(block * width, width), width)
+        loads.append(w_ff_in.at[:, where])
+        loads.append(w_ff_out.at[where, :])
     loads += [join_query, join_key, join_value]
     for k in range(4):
         loads.append(w_ff_out.at[pl.ds(k * width, width), :])
@@ -351,6 +354,12 @@
     def col_over_x(i):
         cross_send(("cx", i), col_ref(2 * i), cols_x.at[0, i], col_x_recv, (0, i), x_mate)
 
+    def half_hidden_over_x(side):
+        where = pl.ds(side * (tokens // 2), tokens // 2)
+        cross_send(
+            ("hx", side), hidden.at[where], cols_x.at[0, 0, where], hidden_x_recv, side, x_mate
+        )
+
     def col_over_y(k):
         source = cols.at[2 + k, :, lanes_of[1]]
         cross_send(("cy", k), source, cols_y.at[0, k], col_y_recv, (0, k), y_mate)
@@ -362,7 +371,8 @@
 
     def pass_col_x(i):
         if ("fx", i) not in cross:
-            need(("cx", i))
+            for key in (("cx", 1),) if i else (("hx", 0), ("hx", 1)):
+                need(key)
             cross_send(
                 ("fx", i), cols_x.at[0, i], cols_x.at[1, i], col_x_recv, (1, i), sibling
             )
@@ -532,6 +542,42 @@
     def fold(value):
         return value.reshape(PIECE // 8, 8, tokens).sum(0)
 
+    banks_in = (adapt_down, adapt_up)
+    half_bank = width // 8
+    far = flip(bn, 2)
+
+    def bank_half(bank, side):
+        return bank.at[pl.ds(pl.multiple_of(side * half_bank, half_bank), half_bank), :]
+
+    bank_y, bank_x, bank_sib = [], [], [[], []]
+
+    def send_bank(source, i, where, kind, mate):
+        return send(
+            source, banks.at[(i, *where)], bank_recv.at[i, kind], mate
+        )
+
+    def pass_from_y(i):
+        bank_y[i].wait_recv()
+        source = banks.at[i, far, x]
+        bank_x.append(send_bank(source, i, (far, x), 3, x_mate))
+        bank_sib[i].append(send_bank(source, i, (far, x), 4, sibling))
+
+    def pass_from_x(i):
+        bank_x[i].wait_recv()
+        source = banks.at[i, far, 1 - x]
+        bank_sib[i].append(send_bank(source, i, (far, 1 - x), 5, sibling))
+
+    def open_links():
+        pl.semaphore_wait(barrier, 1 + len(mates))
+        for i in range(2):
+            bank_y.append(send_bank(bank_half(banks_in[i], x), i, (bn, x), 0, y_mate))
+        for i in range(2):
+            for side in range(2):
+                source = bank_half(banks_in[i], side)
+                bank_sib[i].append(send_bank(source, i, (bn, side), 1 + side, sibling))
+        share_col(0)
+        half_hidden_over_x(0)
+
     length = lengths[0]
     for k in range(3):
         slot = take()
@@ -540,40 +586,8 @@
         if k == 0:
             value = value * 0.125
         qkv_t[pl.ds(k * width, width), :] = value.astype(low).T
-    pl.semaphore_wait(barrier, 1 + len(mates))
-    banks_in = (adapt_down, adapt_up)
-    half_bank = width // 8
-    far = flip(bn, 2)
-
-    def bank_half(bank, side):
-        return bank.at[pl.ds(pl.multiple_of(side * half_bank, half_bank), half_bank), :]
-
-    bank_y, bank_x, bank_sib = [], [], []
-
-    def send_bank(source, i, where, kind, mate):
-        return send(
-            source, banks.at[(i, *where)], bank_recv.at[i, kind], mate
-        )
-
-    for i in range(2):
-        bank_y.append(send_bank(bank_half(banks_in[i], x), i, (bn, x), 0, y_mate))
-    for i in range(2):
-        for side in range(2):
-            source = bank_half(banks_in[i], side)
-            bank_sib.append(send_bank(source, i, (bn, side), 1 + side, sibling))
-
-    def pass_from_y(i):
-        bank_y[i].wait_recv()
-        source = banks.at[i, far, x]
-        bank_x.append(send_bank(source, i, (far, x), 3, x_mate))
-        bank_sib.append(send_bank(source, i, (far, x), 4, sibling))
-
-    def pass_from_x(i):
-        bank_x[i].wait_recv()
-        source = banks.at[i, far, 1 - x]
-        bank_sib.append(send_bank(source, i, (far, 1 - x), 5, sibling))
-
-    share_col(0)
+        if k == 0:
+            open_links()
     size = width // heads
 
     def head_rows(k, head):
@@ -623,7 +637,7 @@
         acc[...] = matmul(cols[1], ring[slot])
         release(slot)
         unit_base = 2 + (k % 2) * 2
-        lanes = pl.ds((k // 2) * half_width, half_width)
+        lanes = lanes_of[1 - k // 2]
 
         def gelu_rows(r, i, carry):
             before = acc[r, :]
@@ -636,19 +650,20 @@
             return carry
 
         over_rows(gelu_rows)
-        slope[pl.ds(k * blocks, blocks)] = cols[9].T.reshape(blocks, PIECE, tokens)
+        slope[pl.ds(ff_blocks[k] * blocks, blocks)] = cols[9].T.reshape(blocks, PIECE, tokens)
         slot = take()
         value = matmul(low_tmp[...], ring[slot])
         release(slot)
         acc_two[...] = value if k == 0 else acc_two[...] + value
         if k == 0:
             pass_from_y(1)
-            for i in range(2):
-                col_over_x(i)
+            half_hidden_over_x(1)
+            col_over_x(1)
+        if k < 2:
+            col_over_y(2 * k)
+            col_over_y(2 * k + 1)
         if k == 2:
             pass_from_x(0)
-    for k in range(4):
-        col_over_y(k)
     for index in range(3, 7):
         share_col(index)
 
@@ -668,7 +683,6 @@
     put_t(3, cols[6].T)
     share_row(3)
 
-    pass_from_x(1)
     slot_query = take()
     low_tmp[...] = matmul(cols[6], ring[slot_query]).astype(low)
     put_t(4, low_tmp[...].T)
@@ -677,11 +691,16 @@
     put_t(2, matmul(ring[slot_key], get_t(4)).astype(low))
     share_row(2)
 
-    for copy in bank_own:
-        copy.wait()
-    for copy in bank_sib:
-        copy.wait_recv()
+    def bank_ready(i):
+        for side in range(2):
+            bank_own[2 * i + side].wait()
+        for copy in bank_sib[i]:
+            copy.wait_recv()
+
+    bank_ready(0)
     acc_t[...] = matmul(banks[0].reshape(width, width), get_t(3)).reshape(blocks, PIECE, tokens)
+    pass_from_x(1)
+    bank_ready(1)
     acc_t_two[...] = matmul(banks[1].reshape(width, width), get_t(2)).reshape(
         blocks, PIECE, tokens
     )
@@ -1034,6 +1053,7 @@
             dma((2, 7)),
             dma((2, 2)),
             dma((2,)),
+            dma((2,)),
             dma((2, 4)),
             dma((4, units)),
             dma((units,)),

time: 116 us -> 112 us (0.966)
  Pallas kernels: 113 us -> 110 us
    pallas_call x1, Pallas kernels: 109 us -> 106 us  [run_layer(): pl.pallas_call(functools.partial(layer_kernel, heads, adapters), out_shap...]
where the time goes in v3:
time: 112 us
  Pallas kernels  110 us (98%)
  between operations  1.48 us (1%)
    pallas_call x1, Pallas kernels, run_layer(): pl.pallas_call(functools.partial(layer_kernel, heads, adapters), out_shap...  106 us
    pallas_call x1, Pallas kernels, finish(): pl.pallas_call(finish_kernel, out_shape=tuple((jax.ShapeDtypeStruct(shape...  4.05 us

profile of v3, /device:TPU:0, one launch (start us, length us, event | category | flops | bytes accessed | tf_op | source)
XLA Modules:
  0.0 111.8 jit_solution(8021321495213978868)
XLA Ops:
  1.3 106.3 %shard_map.254 = (f32[256,768]{1,0:T(8,128)}, f32[256,768]{1,0:T(8,128)}, bf16[17,2,48,384]{3,2,1,0:T(8,128)(2,1)}, f32[8,768]{1,0:T(8,128)}) custom-call(bf16[256,768]{1,0:T(8,128)(2,1)} %hidden.1, s32[1]{0:T(128)S(6)} %copy.29.lengths, bf16[256,768]{1,0:T(8,128)(2,1)} %cotangent_far.1, bf16[768,2304]{1,0:T(8,128)(2,1)} %w_qkv.1, bf16[768,768]{1,0:T(8,128)(2,1)} %w_out.1, ...), custom_call_target="tpu_custom_call" | custom-call | tf_op jit(solution)/shard_map/pallas_call | solution.py:995
  107.6 4.0 %shard_map.255 = (f32[256,768]{1,0:T(8,128)}, f32[256,768]{1,0:T(8,128)}, f32[192,288]{1,0:T(8,128)}, f32[192,96]{1,0:T(8,128)}, f32[96]{0:T(128)}, /*index=5*/f...) custom-call(bf16[17,2,48,384]{3,2,1,0:T(8,128)(2,1)} %get-tuple-elem, ...), custom_call_target="tpu_custom_call" | custom-call | tf_op jit(solution)/shard_map/pallas_call | solution.py:1158

commit v4 on v3

--- a/solution.py
+++ b/solution.py
@@ -605,7 +605,7 @@
         low_tmp_two[pl.ds(pl.multiple_of(head * size, size), size), :] = context.astype(low)
         return carry
 
-    lax.fori_loop(0, heads, head_forward, 0, unroll=3)
+    lax.fori_loop(0, heads, head_forward, 0, unroll=12)
     pass_from_y(0)
     cols[0] = low_tmp_two[...].T
     share_col(1)
@@ -633,9 +633,8 @@
     stat_one[...] = stat[...].T[:8]
 
     for k in range(4):
-        slot = take()
+        slot, slot_two = take(), take()
         acc[...] = matmul(cols[1], ring[slot])
-        release(slot)
         unit_base = 2 + (k % 2) * 2
         lanes = lanes_of[1 - k // 2]
 
@@ -651,10 +650,10 @@
 
         over_rows(gelu_rows)
         slope[pl.ds(ff_blocks[k] * blocks, blocks)] = cols[9].T.reshape(blocks, PIECE, tokens)
-        slot = take()
-        value = matmul(low_tmp[...], ring[slot])
+        value = matmul(low_tmp[...], ring[slot_two])
+        acc_two[...] = value if k == 0 else acc_two[...] + value
         release(slot)
-        acc_two[...] = value if k == 0 else acc_two[...] + value
+        release(slot_two)
         if k == 0:
             pass_from_y(1)
             half_hidden_over_x(1)
@@ -864,9 +863,8 @@
         share_row(6)
 
     def ff_back(k):
-        slot = take()
+        slot, slot_two = take(), take()
         acc_t_two[...] = matmul(ring[slot], get_t(6)).reshape(blocks, PIECE, tokens)
-        release(slot)
 
         def slope_rows(p, carry):
             value = acc_t_two[p] * slope[k * blocks + p].astype(jnp.float32)
@@ -874,10 +872,10 @@
             return carry
 
         over_pieces(slope_rows)
-        slot = take()
-        value = matmul(ring[slot], rows_ff[k].reshape(width, tokens))
+        value = matmul(ring[slot_two], rows_ff[k].reshape(width, tokens))
         value = value.reshape(blocks, PIECE, tokens)
         release(slot)
+        release(slot_two)
         acc_t[...] = value if k == 0 else acc_t[...] + value
         if k == 3:
             for index in range(8, 12):

time: 112 us -> 111 us (level)
    pallas_call x1, Pallas kernels: 106 us -> 105 us  [run_layer(): pl.pallas_call(functools.partial(layer_kernel, heads, adapters), out_shap...]
where the time goes in v4:
time: 111 us
  Pallas kernels  109 us (98%)
  between operations  1.48 us (1%)
    pallas_call x1, Pallas kernels, run_layer(): pl.pallas_call(functools.partial(layer_kernel, heads, adapters), out_shap...  105 us
    pallas_call x1, Pallas kernels, finish(): pl.pallas_call(finish_kernel, out_shape=tuple((jax.ShapeDtypeStruct(shape...  4.05 us

profile of v4, /device:TPU:0, one launch (start us, length us, event | category | flops | bytes accessed | tf_op | source)
XLA Modules:
  0.0 110.7 jit_solution(14931932036472073869)
XLA Ops:
  1.3 105.2 %shard_map.254 = (f32[256,768]{1,0:T(8,128)}, f32[256,768]{1,0:T(8,128)}, bf16[17,2,48,384]{3,2,1,0:T(8,128)(2,1)}, f32[8,768]{1,0:T(8,128)}) custom-call(bf16[256,768]{1,0:T(8,128)(2,1)} %hidden.1, s32[1]{0:T(128)S(6)} %copy.29.lengths, bf16[256,768]{1,0:T(8,128)(2,1)} %cotangent_far.1, bf16[768,2304]{1,0:T(8,128)(2,1)} %w_qkv.1, bf16[768,768]{1,0:T(8,128)(2,1)} %w_out.1, ...), custom_call_target="tpu_custom_call" | custom-call | tf_op jit(solution)/shard_map/pallas_call | solution.py:993
  106.5 4.0 %shard_map.255 = (f32[256,768]{1,0:T(8,128)}, f32[256,768]{1,0:T(8,128)}, f32[192,288]{1,0:T(8,128)}, f32[192,96]{1,0:T(8,128)}, f32[96]{0:T(128)}, /*index=5*/f...) custom-call(bf16[17,2,48,384]{3,2,1,0:T(8,128)(2,1)} %get-tuple-elem, ...), custom_call_target="tpu_custom_call" | custom-call | tf_op jit(solution)/shard_map/pallas_call | solution.py:1156

commit v5 on v4

--- a/solution.py
+++ b/solution.py
@@ -81,7 +81,7 @@
 
 PIECE = 48
 SLOTS = 5
-SENDS = 48
+SENDS = 32
 UNITS = (
     ((0, 8),),
     ((1, 9), (2, 10)),
@@ -682,11 +682,10 @@
     put_t(3, cols[6].T)
     share_row(3)
 
-    slot_query = take()
+    slot_query, slot_key, slot_value = take(), take(), take()
     low_tmp[...] = matmul(cols[6], ring[slot_query]).astype(low)
     put_t(4, low_tmp[...].T)
     share_row(4)
-    slot_key = take()
     put_t(2, matmul(ring[slot_key], get_t(4)).astype(low))
     share_row(2)
 
@@ -743,7 +742,6 @@
 
     over_rows(joined_rows)
     share_col(8)
-    slot_value = take()
     acc[...] = matmul(cols[7], ring[slot_value])
 
     upstream_copy.wait()

time: 111 us -> 111 us (level)
  no operation moved by 1% of the time
where the time goes in v5:
time: 111 us
  Pallas kernels  109 us (98%)
  between operations  1.48 us (1%)
    pallas_call x1, Pallas kernels, run_layer(): pl.pallas_call(functools.partial(layer_kernel, heads, adapters), out_shap...  105 us
    pallas_call x1, Pallas kernels, finish(): pl.pallas_call(finish_kernel, out_shape=tuple((jax.ShapeDtypeStruct(shape...  4.05 us

profile of v5, /device:TPU:0, one launch (start us, length us, event | category | flops | bytes accessed | tf_op | source)
XLA Modules:
  0.0 110.7 jit_solution(2096746460013473115)
XLA Ops:
  1.3 105.1 %shard_map.254 = (f32[256,768]{1,0:T(8,128)}, f32[256,768]{1,0:T(8,128)}, bf16[17,2,48,384]{3,2,1,0:T(8,128)(2,1)}, f32[8,768]{1,0:T(8,128)}) custom-call(bf16[256,768]{1,0:T(8,128)(2,1)} %hidden.1, s32[1]{0:T(128)S(6)} %copy.29.lengths, bf16[256,768]{1,0:T(8,128)(2,1)} %cotangent_far.1, bf16[768,2304]{1,0:T(8,128)(2,1)} %w_qkv.1, bf16[768,768]{1,0:T(8,128)(2,1)} %w_out.1, ...), custom_call_target="tpu_custom_call" | custom-call | tf_op jit(solution)/shard_map/pallas_call | solution.py:991
  106.4 4.0 %shard_map.255 = (f32[256,768]{1,0:T(8,128)}, f32[256,768]{1,0:T(8,128)}, f32[192,288]{1,0:T(8,128)}, f32[192,96]{1,0:T(8,128)}, f32[96]{0:T(128)}, /*index=5*/f...) custom-call(bf16[17,2,48,384]{3,2,1,0:T(8,128)(2,1)} %get-tuple-elem, ...), custom_call_target="tpu_custom_call" | custom-call | tf_op jit(solution)/shard_map/pallas_call | solution.py:1154
